TPU v7x, 128 devices: a whole 4x4x4 slice. The times are simulated.
128 devices in a mesh: day: 2 (over core), region: 16 (over y, x), scen: 4 (over z).
Axes of the slice: x: 4, y: 4, z: 4, core: 2. Of those that a mesh axis runs over, the one named last changes fastest.
Arguments:
- shipments_init: float32 [4, 16, 16, 128, 2, 256], P('scen', 'region', None, None, 'day'), may hold values from 0 to 1
- holdings_init: float32 [4, 1600, 2, 6, 256], P('scen', 'region', 'day'), may hold values from 0 to 2
- selling_init: float32 [4, 1600, 2, 6, 256], P('scen', 'region', 'day'), may hold values from 0 to 1
- shortage_init: float32 [4, 1600, 2, 256], P('scen', 'region', 'day'), may hold values from 0 to 1
- ordering_init: float32 [240, 256], P('region'), may hold values from 0 to 20
- balance_dual_init: float32 [4, 1600, 2, 6, 256], P('scen', 'region', 'day'), may hold values from -3 to 3
- demand_dual_init: float32 [4, 1600, 2, 256], P('scen', 'region', 'day'), may hold values from -3 to 3
- depot_dual_init: float32 [4, 240, 2, 256], P('scen', 'region', 'day'), may hold values from 0 to 0.1
- demand_base: float32 [1600, 256], P('region'), may hold values from 0.5 to 2
- demand_pattern: float32 [16, 256], replicated, may hold values from 0.5 to 2
- demand_index: int32 [4, 1600, 2], P('scen', 'region', 'day'), may hold values from 0 to 15
- initial_stock: float32 [1600, 5, 256], P('region'), may hold values from 0 to 2
- depot_supply: float32 [240, 2, 256], P('region', 'day'), may hold values from 4 to 16
- lane_cost: float32 [16, 16, 128], replicated, may hold values from 0.1 to 1
- item_volume: float32 [256], replicated, may hold values from 0.5 to 2
- holding_cost: float32 [6, 256], replicated, may hold values from 0.05 to 0.5
- unit_price: float32 [256], replicated, may hold values from 1 to 4
- short_penalty: float32 [256], replicated, may hold values from 2 to 8
- order_cost: float32 [256], replicated, may hold values from 0.5 to 2
- lane_depot: int32 [16, 16, 128], replicated, may hold values from 0 to 14
- lane_store: int32 [16, 16, 128], replicated, may hold values from 0 to 99
- lane_mask: int32 [16, 16, 128], replicated, may hold values 0 or 1
Outputs:
- shipments: float32 [4, 16, 16, 128, 2, 256], P('scen', 'region', None, None, 'day')
- holdings: float32 [4, 1600, 2, 6, 256], P('scen', 'region', 'day')
- selling: float32 [4, 1600, 2, 6, 256], P('scen', 'region', 'day')
- ordering: float32 [240, 256], P('region')
- balance_dual: float32 [4, 1600, 2, 6, 256], P('scen', 'region', 'day')
- depot_dual: float32 [4, 240, 2, 256], P('scen', 'region', 'day')
All inputs are finite; a program needn't handle non-finite values.
Results may differ from a plain program's by a relative error of at most 0.0003.
Values sent between devices are 32-bit elements; how exact they have to be, the bound alone decides.
No kernel may reach another device: no remote copies, remote signals or barrier semaphores. Data moves between devices by JAX's collectives and lax.ppermute only.
A program may use at most 128 MiB of HBM per device.

v0:
```python
import functools

import jax
import jax.numpy as jnp
from jax import lax
from jax.experimental import pallas as pl
from jax.experimental.pallas import tpu as pltpu
from jax.sharding import PartitionSpec as P

ITERS = 4
PRIMAL_STEP = 0.25
ORDER_STEP = 0.05
DUAL_STEP = 0.25
DEPOT_STEP = 0.02

REGIONS = 16
DAYS = 2
SCENARIOS = 4
ROWS = DAYS * SCENARIOS
PARTS = REGIONS * ROWS
STORES = 100
QUARTER = STORES // 4
DEPOTS = 15
LANES = 128
AGES = 6
SKUS = 256
HALVES = 2
HOLD, SELL, BAL = 0, AGES, 2 * AGES
MAIN = 3 * AGES
SHORT, DDUAL, DEMAND, STOCK = range(4)
AUX = 4
IN_ROWS = MAIN + REGIONS
OUT_MAIN = 15
OUT_ROWS = OUT_MAIN + REGIONS
SPARE = STORES
HOSTS = {
    SHORT: (HOLD, HOLD + 1, HOLD + 2, HOLD + 3),
    DDUAL: (SELL, SELL + 1, SELL + 2, SELL + 3),
    DEMAND: (BAL, BAL + 1, BAL + 2, BAL + 3),
    STOCK: (HOLD + 4, HOLD + 5, SELL + 4, SELL + 5),
}
DUAL_HOST, MIXED_HOST = BAL + 4, BAL + 5
OUT_DUAL_HOST, OUT_ORDER_HOST = 12, 13
DEPOT_COLUMN = 112
DEPOT_PITCH = 16
GROUP = 8
VOLUME, PRICE, PENALTY, ORDER_COST, HOLDING_COST = range(5)

VMEM_BYTES = 20 * 1024 * 1024
f32 = jnp.float32
VM = pl.BlockSpec(memory_space=pltpu.VMEM)
SM = pl.BlockSpec(memory_space=pltpu.SMEM)
HB = pl.BlockSpec(memory_space=pltpu.HBM)
EVERY = ("region", "day", "scen")


def call(body, outs, specs, out_specs, scratch=(), micros=1):
    return pl.pallas_call(
        body,
        out_shape=outs,
        in_specs=specs,
        out_specs=out_specs,
        scratch_shapes=list(scratch),
        compiler_params=pltpu.CompilerParams(vmem_limit_bytes=VMEM_BYTES),
        cost_estimate=pl.CostEstimate(
            flops=micros * 500_000_000, bytes_accessed=micros * 3_000_000, transcendentals=0
        ),
    )


def in_hbm(array):
    return pltpu.with_memory_space_constraint(array, pltpu.HBM)


def in_vmem(array):
    return pltpu.with_memory_space_constraint(array, pltpu.VMEM)


def lane_window(start, size):
    lane = lax.broadcasted_iota(jnp.int32, (ROWS, LANES), 1)
    return (lane >= start) & (lane < start + size)


def shift_lanes(x, source, target):
    return pltpu.roll(x, (target - source) % LANES, 1)


def other_day(x):
    return pltpu.roll(x, SCENARIOS, 0)


def pack_kernel(half, place_ref, *refs):
    given, out_ref, held = refs[:13], refs[13], refs[14:27]
    packed, rows, index, came, left = refs[27:]
    (
        ship_ref,
        hold_ref,
        sell_ref,
        bal_ref,
        short_ref,
        ddual_ref,
        base_ref,
        pattern_ref,
        index_ref,
        stock_ref,
        depot_dual_ref,
        ordering_ref,
        supply_ref,
    ) = held
    coming = [pltpu.make_async_copy(given[i], held[i], came.at[i]) for i in range(13)]
    for copy in coming:
        copy.start()
    scen = place_ref[1]
    place = place_ref[0] * SCENARIOS + scen
    cols = slice(half * LANES, (half + 1) * LANES)

    coming[0].wait()

    def ship_step(b, carry):
        lanes = ship_ref[pl.ds(b * (2 * LANES) + half, LANES, stride=2), :]
        packed[pl.ds(MAIN + b, PARTS, stride=IN_ROWS), :] = lanes.T
        return carry

    lax.fori_loop(0, REGIONS, ship_step, 0)
    for copy in coming[1:]:
        copy.wait()
    index[...] = jnp.zeros_like(index)
    index[0:1, 0:STORES] = index_ref[...]
    patterns = pattern_ref.shape[0]
    chosen = lax.broadcasted_iota(jnp.int32, (patterns, LANES), 0) == index[0:1, :]
    factor = lax.dot_general(
        chosen.astype(f32),
        pattern_ref[:, cols],
        (((0,), (0,)), ((), ())),
        precision=lax.Precision.HIGHEST,
        preferred_element_type=f32,
    )
    demand = factor[0:STORES] * base_ref[:, cols]
    stock = stock_ref.at[jnp.minimum(place, AGES - 2)]

    def quarter(kind, q):
        first = QUARTER * q
        if kind == DEMAND:
            return demand[first : first + QUARTER]
        if kind == STOCK:
            return stock[first : first + QUARTER, cols]
        ref = short_ref if kind == SHORT else ddual_ref
        return ref[pl.ds(2 * first + half, QUARTER, stride=2), :]

    for slot in range(MAIN):
        ref, age = (hold_ref, sell_ref, bal_ref)[slot // AGES], slot % AGES
        block = rows.at[slot]
        block[96:LANES, :] = jnp.zeros((LANES - 96, LANES), f32)
        block[0:STORES, :] = ref[pl.ds(2 * age + half, STORES, stride=2 * AGES), :]
        for kind, hosts in HOSTS.items():
            if slot in hosts:
                block[SPARE : SPARE + QUARTER, :] = quarter(kind, hosts.index(slot))
        if slot == DUAL_HOST:
            block[SPARE : SPARE + DEPOTS, :] = depot_dual_ref[:, 0, cols]
        if slot == MIXED_HOST:
            block[SPARE : SPARE + DEPOTS, :] = jnp.where(
                scen % 2 == 0, supply_ref[:, 0, cols], ordering_ref[:, cols]
            )
        packed[pl.ds(slot, PARTS, stride=IN_ROWS), :] = block[...].T
    going = pltpu.make_async_copy(packed, out_ref, left)
    going.start()
    going.wait()


def unpack_kernel(half, in_ref, *refs):
    count = 6
    given = refs[: count * half]
    outs = refs[count * half : count * (half + 1)]
    held = refs[count * (half + 1) : count * (half + 2)]
    *earlier, came, left = refs[count * (half + 2) :]
    ship_ref, hold_ref, sell_ref, bal_ref, depot_dual_ref, ordering_ref = held
    coming = [pltpu.make_async_copy(given[i], earlier[i], came.at[i]) for i in range(len(given))]
    for copy in coming:
        copy.start()
    going = [pltpu.make_async_copy(held[i], outs[i], left.at[i]) for i in range(count)]
    pace = half + 1

    def get(slot):
        return in_ref[pl.ds(slot, PARTS, stride=OUT_ROWS), :].T

    if half:
        coming[0].wait()

    def ship_step(b, carry):
        ship_ref[pl.ds(b * (LANES * pace) + half, LANES, stride=pace), :] = get(OUT_MAIN + b)
        if half:
            ship_ref[pl.ds(b * (LANES * pace), LANES, stride=pace), :] = earlier[0][
                pl.ds(b * LANES, LANES), :
            ]
        return carry

    lax.fori_loop(0, REGIONS, ship_step, 0)
    going[0].start()
    for copy in coming[1:]:
        copy.wait()
    if half:
        for i, ref in ((1, hold_ref), (2, sell_ref), (3, bal_ref)):
            ref[pl.ds(0, STORES * AGES, stride=2), :] = earlier[i][...]
        depot_dual_ref[:, 0, :LANES] = earlier[4][...]
        ordering_ref[:, :LANES] = earlier[5][...]
    for slot in range(OUT_MAIN):
        ref, age = (hold_ref, sell_ref, bal_ref)[slot // AGES], slot % AGES
        rows = get(slot)
        ref[pl.ds(pace * age + half, STORES, stride=pace * AGES), :] = rows[0:STORES]
        if slot < 12:
            at = pace * (AGES * QUARTER * (slot % 4) + 3 + slot // 4) + half
            bal_ref[pl.ds(at, QUARTER, stride=pace * AGES), :] = rows[SPARE : SPARE + QUARTER]
        depots = rows[SPARE : SPARE + DEPOTS]
        if slot == OUT_DUAL_HOST:
            if half:
                depot_dual_ref[:, 0, LANES:] = depots
            else:
                depot_dual_ref[...] = depots
        if slot == OUT_ORDER_HOST:
            if half:
                ordering_ref[:, LANES:] = depots
            else:
                ordering_ref[...] = depots
    for copy in going[1:]:
        copy.start()
    for copy in going:
        copy.wait()


def tables_kernel(
    place_ref, store_ref, depot_ref, mask_ref, table_ref, slot_ref, keep_ref, next_ref
):
    for i in range(2):
        next_ref[i] = place_ref[i]
    column = lax.broadcasted_iota(jnp.int32, (LANES, LANES), 0)

    def step(b, carry):
        for a in range(REGIONS):
            keep = mask_ref[a, pl.ds(b, 1), :] > 0
            store = jnp.where(keep, store_ref[a, pl.ds(b, 1), :], -1)
            depot = jnp.where(keep, depot_ref[a, pl.ds(b, 1), :] + DEPOT_COLUMN, -1)
            ends = (column == store) | (column == depot)
            table_ref[b, a] = jnp.where(ends, 1.0, 0.0).astype(f32).T.astype(jnp.bfloat16)
        return carry

    lax.fori_loop(0, REGIONS, step, 0)
    for a in range(REGIONS):
        slot_ref[a] = depot_ref[a] + (a % GROUP) * DEPOT_PITCH
        keep_ref[a] = mask_ref[a].astype(f32)


def iterations_kernel(
    in_ref,
    number_ref,
    table_ref,
    store_ref,
    slot_ref,
    cost_ref,
    keep_ref,
    out_ref,
    ship,
    main,
    aux,
    flow,
    dual,
    ordering,
    supply,
    packed,
    left,
):
    sublane = lax.broadcasted_iota(jnp.int32, (ROWS, LANES), 0)
    first_day = sublane < SCENARIOS
    even = sublane % 2 == 0
    zero = jnp.zeros((ROWS, LANES), f32)
    quarters = [lane_window(QUARTER * q, QUARTER) for q in range(4)]
    spares = lane_window(SPARE, QUARTER)
    depot_spares = lane_window(SPARE, DEPOTS)

    def unfold(region, carry):
        at = region * (ROWS * IN_ROWS)
        for slot in range(MAIN):
            main[region, slot] = in_ref[pl.ds(at + slot, ROWS, stride=IN_ROWS), :]
        for b in range(REGIONS):
            ship[region, b] = in_ref[pl.ds(at + MAIN + b, ROWS, stride=IN_ROWS), :]
        for kind, hosts in HOSTS.items():
            total = zero
            for q in range(4):
                part = shift_lanes(main[region, hosts[q]], SPARE, QUARTER * q)
                total = jnp.where(quarters[q], part, total)
            aux[region, kind] = total
        return carry

    lax.fori_loop(0, REGIONS, unfold, 0)
    for group in range(2):
        duals, mixed = zero, zero
        for i in range(GROUP):
            region, at = group * GROUP + i, i * DEPOT_PITCH
            window = lane_window(at, DEPOTS)
            duals = jnp.where(window, shift_lanes(main[region, DUAL_HOST], SPARE, at), duals)
            mixed = jnp.where(window, shift_lanes(main[region, MIXED_HOST], SPARE, at), mixed)
        dual[group] = duals
        supply[group] = jnp.where(even, mixed, pltpu.roll(mixed, 1, 0))
        ordering[group] = jnp.where(even, pltpu.roll(mixed, ROWS - 1, 0), mixed)

    volume, price, penalty, order_cost = (number_ref[i] for i in range(4))
    holding_cost = [number_ref[HOLDING_COST + age] for age in range(AGES)]

    def iterate(iteration, carry):
        flow[...] = jnp.zeros_like(flow)
        later = [
            dual[group] + jnp.where(first_day, other_day(dual[group]), 0.0) for group in range(2)
        ]

        def step(b, carry):
            bal = [main[b, BAL + age] for age in range(AGES)]
            ddual, short = aux[b, DDUAL], aux[b, SHORT]
            new_short = jnp.maximum(0.0, short - PRIMAL_STEP * (penalty - ddual))
            aux[b, SHORT] = new_short
            sold, before, ended = zero, None, None
            for age in range(AGES):
                hold, sell = main[b, HOLD + age], main[b, SELL + age]
                rise = holding_cost[age] - bal[age]
                if age + 1 < AGES:
                    rise = rise + jnp.where(first_day, other_day(bal[age + 1]), 0.0)
                new_hold = jnp.maximum(0.0, hold - PRIMAL_STEP * rise)
                new_sell = jnp.maximum(0.0, sell - PRIMAL_STEP * (-price - bal[age] - ddual))
                main[b, HOLD + age] = new_hold
                main[b, SELL + age] = new_sell
                hold_bar = 2.0 * new_hold - hold
                sell_bar = 2.0 * new_sell - sell
                sold = sold + sell_bar
                if age == 0:
                    ended = bal[0] - DUAL_STEP * (hold_bar + sell_bar)
                else:
                    stock = jnp.broadcast_to(aux[b, STOCK, age - 1 : age, :], (ROWS, LANES))
                    carried = jnp.where(first_day, stock, other_day(before))
                    main[b, BAL + age] = bal[age] - DUAL_STEP * (hold_bar + sell_bar - carried)
                before = hold_bar
            short_bar = 2.0 * new_short - short
            aux[b, DDUAL] = ddual + DUAL_STEP * (aux[b, DEMAND] - sold - short_bar)
            arrived = zero
            for a in range(REGIONS):
                def spread(ref):
                    return jnp.broadcast_to(ref[a, pl.ds(b, 1), :], (ROWS, LANES))

                ends = jnp.take_along_axis(
                    bal[0], spread(store_ref), axis=1, mode="promise_in_bounds"
                ) + jnp.take_along_axis(
                    later[a // GROUP], spread(slot_ref), axis=1, mode="promise_in_bounds"
                )
                old = ship[a, b]
                new = spread(keep_ref) * jnp.maximum(
                    0.0, old - PRIMAL_STEP * (spread(cost_ref) * volume + ends)
                )
                ship[a, b] = new
                bar = 2.0 * new - old
                high = bar.astype(jnp.bfloat16).astype(f32)
                parts = jnp.concatenate([high, bar - high], axis=0).astype(jnp.bfloat16)
                sums = jnp.dot(parts, table_ref[b, a], preferred_element_type=f32)
                sums = sums[:ROWS] + sums[ROWS:]
                flow[a] = flow[a] + sums
                arrived = arrived + sums
            main[b, BAL] = ended + DUAL_STEP * arrived
            return carry

        lax.fori_loop(0, REGIONS, step, 0)
        for group in range(2):
            total = dual[group]
            for shift in (4, 2, 1):
                total = total + pltpu.roll(total, shift, 0)
            old = ordering[group]
            new = jnp.maximum(0.0, old - ORDER_STEP * (order_cost - total))
            ordering[group] = new
            net = -supply[group]
            for i in range(GROUP):
                at = i * DEPOT_PITCH
                part = shift_lanes(flow[group * GROUP + i], DEPOT_COLUMN, at)
                net = net + jnp.where(lane_window(at, DEPOTS), part, 0.0)
            running = net + jnp.where(first_day, 0.0, other_day(net))
            dual[group] = jnp.maximum(
                0.0, dual[group] + DEPOT_STEP * (running - (2.0 * new - old))
            )
        return carry

    lax.fori_loop(0, ITERS, iterate, 0)

    def fold(region, carry):
        at = region * (ROWS * OUT_ROWS)
        for slot in range(OUT_MAIN):
            tile = main[region, slot]
            if slot < 12:
                hosted = main[region, BAL + 3 + slot // 4]
                hosted = shift_lanes(hosted, QUARTER * (slot % 4), SPARE)
                tile = jnp.where(spares, hosted, tile)
            packed[pl.ds(at + slot, ROWS, stride=OUT_ROWS), :] = tile
        for b in range(REGIONS):
            packed[pl.ds(at + OUT_MAIN + b, ROWS, stride=OUT_ROWS), :] = ship[region, b]
        return carry

    lax.fori_loop(0, REGIONS, fold, 0)
    for group in range(2):
        for i in range(GROUP):
            region = group * GROUP + i
            at = region * (ROWS * OUT_ROWS)
            for host, ref in ((OUT_DUAL_HOST, dual), (OUT_ORDER_HOST, ordering)):
                part = shift_lanes(ref[group], i * DEPOT_PITCH, SPARE)
                packed[pl.ds(at + host, ROWS, stride=OUT_ROWS), :] = jnp.where(
                    depot_spares, part, main[region, host]
                )
    going = pltpu.make_async_copy(packed, out_ref, left)
    going.start()
    going.wait()


def swap(rows):
    parts = rows.reshape(PARTS, -1, 1, LANES)
    return lax.all_to_all(parts, EVERY, 0, 0, tiled=True).reshape(-1, LANES)


def per_device(
    shipments_init,
    holdings_init,
    selling_init,
    shortage_init,
    ordering_init,
    balance_dual_init,
    demand_dual_init,
    depot_dual_init,
    demand_base,
    demand_pattern,
    demand_index,
    initial_stock,
    depot_supply,
    lane_cost,
    item_volume,
    holding_cost,
    unit_price,
    short_penalty,
    order_cost,
    lane_depot,
    lane_store,
    lane_mask,
):
    place = jnp.stack([lax.axis_index("day"), lax.axis_index("scen")]).astype(jnp.int32)
    given = (
        shipments_init.reshape(-1, LANES),
        holdings_init.reshape(-1, LANES),
        selling_init.reshape(-1, LANES),
        balance_dual_init.reshape(-1, LANES),
        shortage_init.reshape(-1, LANES),
        demand_dual_init.reshape(-1, LANES),
        demand_base,
        demand_pattern,
        demand_index.reshape(1, STORES),
        jnp.transpose(initial_stock, (1, 0, 2)),
        depot_dual_init.reshape(DEPOTS, 1, SKUS),
        ordering_init,
        depot_supply,
    )
    arrived = []
    for half in range(HALVES):
        packed = call(
            functools.partial(pack_kernel, half),
            pltpu.HBM((PARTS * IN_ROWS, LANES), f32),
            [SM] + [HB] * len(given),
            HB,
            scratch=[
                *(pltpu.VMEM(array.shape, array.dtype) for array in given),
                pltpu.VMEM((PARTS * IN_ROWS, LANES), f32),
                pltpu.VMEM((MAIN, LANES, LANES), f32),
                pltpu.VMEM((8, LANES), jnp.int32),
                pltpu.SemaphoreType.DMA((len(given),)),
                pltpu.SemaphoreType.DMA,
            ],
            micros=4,
        )(place, *(in_hbm(array) for array in given))
        arrived.append(swap(packed))
        if half == 0:
            slots = (REGIONS, REGIONS, LANES)
            table, slot, keep, place = call(
                tables_kernel,
                (
                    pltpu.VMEM((REGIONS, REGIONS, LANES, LANES), jnp.bfloat16),
                    pltpu.VMEM(slots, jnp.int32),
                    pltpu.VMEM(slots, f32),
                    jax.ShapeDtypeStruct((2,), jnp.int32),
                ),
                [SM, VM, VM, VM],
                (VM, VM, VM, SM),
                micros=5,
            )(place, lane_store, lane_depot, lane_mask)
    numbers = jnp.concatenate(
        [jnp.stack([item_volume, unit_price, short_penalty, order_cost]), holding_cost], axis=0
    )
    own = (lax.axis_index("region") * DAYS + lax.axis_index("day")) * SCENARIOS
    own = own + lax.axis_index("scen")
    back = []
    for half in range(HALVES):
        mine = lax.dynamic_slice(numbers, (0, half * LANES + own), (numbers.shape[0], 1))
        back.append(
            swap(
                call(
                    iterations_kernel,
                    pltpu.HBM((PARTS * OUT_ROWS, LANES), f32),
                    [VM, SM] + [VM] * 5,
                    HB,
                    scratch=[
                        pltpu.VMEM((REGIONS, REGIONS, ROWS, LANES), f32),
                        pltpu.VMEM((REGIONS, MAIN, ROWS, LANES), f32),
                        pltpu.VMEM((REGIONS, AUX, ROWS, LANES), f32),
                        pltpu.VMEM((REGIONS, ROWS, LANES), f32),
                        pltpu.VMEM((2, ROWS, LANES), f32),
                        pltpu.VMEM((2, ROWS, LANES), f32),
                        pltpu.VMEM((2, ROWS, LANES), f32),
                        pltpu.VMEM((PARTS * OUT_ROWS, LANES), f32),
                        pltpu.SemaphoreType.DMA,
                    ],
                    micros=20,
                )(
                    arrived[half],
                    mine.reshape(-1),
                    in_vmem(table),
                    lane_store,
                    in_vmem(slot),
                    lane_cost,
                    in_vmem(keep),
                )
            )
        )
    done = ()
    for half in range(HALVES):
        pace = half + 1
        flat = (STORES * pace * AGES, LANES)
        shapes = (
            (pace * REGIONS * LANES, LANES),
            flat,
            flat,
            flat,
            (DEPOTS, 1, SKUS) if half else (DEPOTS, LANES),
            (DEPOTS, pace * LANES),
        )
        count = len(shapes)
        done = call(
            functools.partial(unpack_kernel, half),
            tuple(pltpu.HBM(shape, f32) for shape in shapes),
            [VM] + [HB] * len(done),
            (HB,) * count,
            scratch=[
                *(pltpu.VMEM(shape, f32) for shape in shapes),
                *(pltpu.VMEM(array.shape, f32) for array in done),
                pltpu.SemaphoreType.DMA((count,)),
                pltpu.SemaphoreType.DMA((count,)),
            ],
            micros=4,
        )(back[half], *(in_hbm(array) for array in done))
    shipments, holdings, selling, balance, depot_dual, ordering = done
    return (
        shipments.reshape(1, 1, REGIONS, LANES, 1, SKUS),
        holdings.reshape(1, STORES, 1, AGES, SKUS),
        selling.reshape(1, STORES, 1, AGES, SKUS),
        ordering,
        balance.reshape(1, STORES, 1, AGES, SKUS),
        depot_dual.reshape(1, DEPOTS, 1, SKUS),
    )


def solution(mesh):
    placed = (
        P("scen", "region", None, None, "day", None),
        P("scen", "region", "day", None, None),
        P("scen", "region", "day", None, None),
        P("scen", "region", "day", None),
        P("region", None),
        P("scen", "region", "day", None, None),
        P("scen", "region", "day", None),
        P("scen", "region", "day", None),
        P("region", None),
        P(),
        P("scen", "region", "day"),
        P("region", None, None),
        P("region", "day", None),
        P(),
        P(),
        P(),
        P(),
        P(),
        P(),
        P(),
        P(),
        P(),
    )
    return jax.shard_map(
        per_device,
        mesh=mesh,
        in_specs=placed,
        out_specs=(
            P("scen", "region", None, None, "day", None),
            P("scen", "region", "day", None, None),
            P("scen", "region", "day", None, None),
            P("region", None),
            P("scen", "region", "day", None, None),
            P("scen", "region", "day", None),
        ),
        check_vma=False,
    )
```

profile of v0, /device:TPU:1, one launch (start us, length us, event | category | flops | bytes accessed | tf_op | source)
XLA Modules:
  0.0 171.9 jit_solution(8168667154542192476)
XLA Ops:
  0.6 0.1 pad_add_fusion.place_ref
  0.7 5.8 %shard_map.256 = f32[4352,128]{1,0:T(8,128)} custom-call(s32[2]{0:T(128)S(1)} %pad_add_fusion.place_ref, f32[4096,128]{1,0:T(8,128)} %bitcast.38, f32[1200,128]{1,0:T(8,128)} %bitcast.40, f32[1200,128]{1,0:T(8,128)} %bitcast.42, f32[1200,128]{1,0:T(8,128)} %bitcast.44, f32[200,128]{1,0:T(8,128)} %bitcast.48, f32[200,128]{1,0:T(8,128)} %bitcast.50, ...), custom_call_target="tpu_custom_call" | custom-call | flops 2000000000 | bytes 12000000 | tf_op jit(solution)/shard_map/pallas_call | solution.py:462
  6.5 0.0 copy-start
  6.5 0.0 copy-start.1
  6.5 0.0 copy-start.2
  6.5 11.5 %all-to-all-start.2 = ((f32[128,34,1,128]{3,2,1,0:T(1,128)}), f32[128,34,1,128]{3,2,1,0:T(1,128)S(1)}, u32[]{:S(2)}, u32[]{:S(2)}) async-start(f32[128,34,1,128]{3,2,1,0:T(1,128)} %bitcast.31), calls=%async_computation.2 | async-start | bytes 4456448 | tf_op jit(solution)/shard_map/all_to_all | solution.py:417
  18.0 0.0 copy-done
  18.0 0.0 copy-done.1
  18.0 0.0 copy-done.2
  18.1 5.0 %shard_map.253 = (bf16[16,16,128,128]{3,2,1,0:T(8,128)(2,1)S(1)}, s32[16,16,128]{2,1,0:T(8,128)S(1)}, f32[16,16,128]{2,1,0:T(8,128)S(1)}, s32[2]{0:T(128)S(1)}) custom-call(s32[2]{0:T(128)S(1)} %pad_add_fusion.place_ref, s32[16,16,128]{2,1,0:T(8,128)S(1)} %copy-done.2, s32[16,16,128]{2,1,0:T(8,128)S(1)} %copy-done, s32[16,16,128]{2,1,0:T(8,128)S(1)} %copy-done.1), custom_call_target="tpu_custom_call" | custom-call | flops 2500000000 | bytes 15000000 | tf_op jit(solution)/shard_map/pallas_call | solution.py:480
  23.0 0.0 copy-start.4
  23.0 3.2 %copy-done.4 = bf16[16,16,128,128]{3,2,1,0:T(8,128)(2,1)} copy-done((bf16[16,16,128,128]{3,2,1,0:T(8,128)(2,1)}, bf16[16,16,128,128]{3,2,1,0:T(8,128)(2,1)S(1)}, u32[]{:S(2)}) %copy-start.4) | copy-done | bytes 8388632
  26.3 5.7 %shard_map.254 = f32[4352,128]{1,0:T(8,128)} custom-call(s32[2]{0:T(128)S(1)} %get-tuple-element.22.place_ref, f32[4096,128]{1,0:T(8,128)} %bitcast.39, f32[1200,128]{1,0:T(8,128)} %bitcast.41, f32[1200,128]{1,0:T(8,128)} %bitcast.43, f32[1200,128]{1,0:T(8,128)} %bitcast.45, f32[200,128]{1,0:T(8,128)} %bitcast.49, f32[200,128]{1,0:T(8,128)} %bitcast.51, ...), custom_call_target="tpu_custom_call" | custom-call | flops 2000000000 | bytes 12000000 | tf_op jit(solution)/shard_map/pallas_call | solution.py:462
  32.0 18.0 %all-to-all-done.2 = f32[128,34,1,128]{3,2,1,0:T(1,128)S(1)} async-done(((f32[128,34,1,128]{3,2,1,0:T(1,128)}), f32[128,34,1,128]{3,2,1,0:T(1,128)S(1)}, u32[]{:S(2)}, u32[]{:S(2)}) %all-to-all-start.2) | async-done | bytes 2228256 | tf_op jit(solution)/shard_map/all_to_all | solution.py:417
  50.0 0.0 copy-start.7
  50.0 0.0 copy-start.8
  50.0 0.0 copy-start.9
  50.0 0.0 copy-start.10
  50.0 0.0 copy-start.11
  50.0 0.0 copy-start.3
  50.0 4.9 %all-to-all-start = ((f32[128,34,1,128]{3,2,1,0:T(1,128)}), f32[128,34,1,128]{3,2,1,0:T(1,128)}, u32[]{:S(2)}, u32[]{:S(2)}) async-start(f32[128,34,1,128]{3,2,1,0:T(1,128)} %bitcast.30), calls=%async_computation | async-start | bytes 4456448 | tf_op jit(solution)/shard_map/all_to_all | solution.py:417
  54.9 0.0 copy-done.7
  54.9 0.0 copy-done.8
  55.0 0.0 copy-done.9
  55.0 0.0 copy-done.10
  55.0 0.0 copy-done.11
  55.0 0.1 concatenate.3
  55.1 0.2 dynamic-slice_reduce_fusion
  55.3 0.0 copy-done.3
  55.3 0.0 copy-start.5
  55.3 3.4 %copy-done.5 = bf16[16,16,128,128]{3,2,1,0:T(8,128)(2,1)S(1)} copy-done((bf16[16,16,128,128]{3,2,1,0:T(8,128)(2,1)S(1)}, bf16[16,16,128,128]{3,2,1,0:T(8,128)(2,1)}, u32[]{:S(2)}) %copy-start.5) | copy-done | bytes 8388632
  58.7 26.3 %shard_map.257 = f32[3968,128]{1,0:T(8,128)} custom-call(f32[4352,128]{1,0:T(8,128)S(1)} %bitcast.28, f32[10]{0:T(128)S(1)} %get-tuple-element.56.number_ref, bf16[16,16,128,128]{3,2,1,0:T(8,128)(2,1)S(1)} %copy-done.5, s32[16,16,128]{2,1,0:T(8,128)S(1)} %copy-done.2, s32[16,16,128]{2,1,0:T(8,128)S(1)} %get-tuple-element.24.slot_ref, ...), custom_call_target="tpu_custom_call" | custom-call | flops 10000000000 | bytes 60000000 | tf_op jit(solution)/shard_map/pallas_call | solution.py:502
  85.0 1.7 %all-to-all-done = f32[128,34,1,128]{3,2,1,0:T(1,128)} async-done(((f32[128,34,1,128]{3,2,1,0:T(1,128)}), f32[128,34,1,128]{3,2,1,0:T(1,128)}, u32[]{:S(2)}, u32[]{:S(2)}) %all-to-all-start) | async-done | bytes 2228256 | tf_op jit(solution)/shard_map/all_to_all | solution.py:417
  86.7 8.2 %all-to-all-start.3 = ((f32[128,31,1,128]{3,2,1,0:T(1,128)}), f32[128,31,1,128]{3,2,1,0:T(1,128)S(1)}, u32[]{:S(2)}, u32[]{:S(2)}) async-start(f32[128,31,1,128]{3,2,1,0:T(1,128)} %bitcast.33), calls=%async_computation.3 | async-start | bytes 4063232 | tf_op jit(solution)/shard_map/all_to_all | solution.py:417
  94.9 0.0 copy-start.6
  94.9 3.4 %copy-done.6 = bf16[16,16,128,128]{3,2,1,0:T(8,128)(2,1)S(1)} copy-done((bf16[16,16,128,128]{3,2,1,0:T(8,128)(2,1)S(1)}, bf16[16,16,128,128]{3,2,1,0:T(8,128)(2,1)}, u32[]{:S(2)}) %copy-start.6) | copy-done | bytes 8388632
  98.3 27.4 %shard_map.255 = f32[3968,128]{1,0:T(8,128)} custom-call(f32[4352,128]{1,0:T(8,128)} %bitcast.12.in_ref, f32[10]{0:T(128)S(1)} %get-tuple-element.57.number_ref, bf16[16,16,128,128]{3,2,1,0:T(8,128)(2,1)S(1)} %copy-done.6, s32[16,16,128]{2,1,0:T(8,128)S(1)} %copy-done.2, s32[16,16,128]{2,1,0:T(8,128)S(1)} %get-tuple-element.24.slot_ref, ...), custom_call_target="tpu_custom_call" | custom-call | flops 10000000000 | bytes 60000000 | tf_op jit(solution)/shard_map/pallas_call | solution.py:502
  125.7 0.0 all-to-all-done.3
  125.7 10.2 %all-to-all-start.1 = ((f32[128,31,1,128]{3,2,1,0:T(1,128)}), f32[128,31,1,128]{3,2,1,0:T(1,128)}, u32[]{:S(2)}, u32[]{:S(2)}) async-start(f32[128,31,1,128]{3,2,1,0:T(1,128)} %bitcast.32), calls=%async_computation.1 | async-start | bytes 4063232 | tf_op jit(solution)/shard_map/all_to_all | solution.py:417
  135.9 3.0 %shard_map.258 = (f32[2048,128]{1,0:T(8,128)}, f32[600,128]{1,0:T(8,128)}, f32[600,128]{1,0:T(8,128)}, f32[600,128]{1,0:T(8,128)}, f32[15,128]{1,0:T(8,128)}, /*index=5*/f32[15,128]{1,0:T(8,128)}) custom-call(f32[3968,128]{1,0:T(8,128)S(1)} %bitcast.29), custom_call_target="tpu_custom_call" | custom-call | flops 2000000000 | bytes 12000000 | tf_op jit(solution)/shard_map/pallas_call | solution.py:543
  138.9 26.6 %all-to-all-done.1 = f32[128,31,1,128]{3,2,1,0:T(1,128)} async-done(((f32[128,31,1,128]{3,2,1,0:T(1,128)}), f32[128,31,1,128]{3,2,1,0:T(1,128)}, u32[]{:S(2)}, u32[]{:S(2)}) %all-to-all-start.1) | async-done | bytes 2031648 | tf_op jit(solution)/shard_map/all_to_all | solution.py:417
  165.5 6.4 %shard_map.259 = (f32[4096,128]{1,0:T(8,128)}, f32[1200,128]{1,0:T(8,128)}, f32[1200,128]{1,0:T(8,128)}, f32[1200,128]{1,0:T(8,128)}, f32[15,1,256]{2,1,0:T(1,128)}, /*index=5*/f32[15,256]{1,0:T(8,128)}) custom-call(f32[3968,128]{1,0:T(8,128)} %bitcast.18.in_ref, f32[2048,128]{1,0:T(8,128)} %get-tuple-element.26.refs_0_, ...), custom_call_target="tpu_custom_call" | custom-call | flops 2000000000 | bytes 12000000 | tf_op jit(solution)/shard_map/pallas_call | solution.py:543
Async XLA Ops:
  6.5 11.5 %copy-start = (s32[16,16,128]{2,1,0:T(8,128)S(1)}, s32[16,16,128]{2,1,0:T(8,128)}, u32[]{:S(2)}) copy-start(s32[16,16,128]{2,1,0:T(8,128)} %depot_ref.1) | copy-start | bytes 393220
  6.5 11.5 %copy-start.1 = (s32[16,16,128]{2,1,0:T(8,128)S(1)}, s32[16,16,128]{2,1,0:T(8,128)}, u32[]{:S(2)}) copy-start(s32[16,16,128]{2,1,0:T(8,128)} %mask_ref.1) | copy-start | bytes 393220
  6.5 11.5 %copy-start.2 = (s32[16,16,128]{2,1,0:T(8,128)S(1)}, s32[16,16,128]{2,1,0:T(8,128)}, u32[]{:S(2)}) copy-start(s32[16,16,128]{2,1,0:T(8,128)} %store_ref.5) | copy-start | bytes 393220
  6.5 43.5 %all-to-all-start.2 = ((f32[128,34,1,128]{3,2,1,0:T(1,128)}), f32[128,34,1,128]{3,2,1,0:T(1,128)S(1)}, u32[]{:S(2)}, u32[]{:S(2)}) async-start(f32[128,34,1,128]{3,2,1,0:T(1,128)} %bitcast.31), calls=%async_computation.2 | async-start | bytes 4456448 | tf_op jit(solution)/shard_map/all_to_all | solution.py:417
  23.0 3.2 %copy-start.4 = (bf16[16,16,128,128]{3,2,1,0:T(8,128)(2,1)}, bf16[16,16,128,128]{3,2,1,0:T(8,128)(2,1)S(1)}, u32[]{:S(2)}) copy-start(bf16[16,16,128,128]{3,2,1,0:T(8,128)(2,1)S(1)} %get-tuple-element.23.table_ref) | copy-start | bytes 25165828
  50.0 5.0 %copy-start.7 = (f32[6,256]{1,0:T(8,128)S(1)}, f32[6,256]{1,0:T(8,128)}, u32[]{:S(2)}) copy-start(f32[6,256]{1,0:T(8,128)} %param.37) | copy-start | bytes 18436
  50.0 5.0 %copy-start.8 = (f32[256]{0:T(256)S(1)}, f32[256]{0:T(256)}, u32[]{:S(2)}) copy-start(f32[256]{0:T(256)} %param.36) | copy-start | bytes 3076
  50.0 5.0 %copy-start.9 = (f32[256]{0:T(256)S(1)}, f32[256]{0:T(256)}, u32[]{:S(2)}) copy-start(f32[256]{0:T(256)} %param.38) | copy-start | bytes 3076
  50.0 5.0 %copy-start.10 = (f32[256]{0:T(256)S(1)}, f32[256]{0:T(256)}, u32[]{:S(2)}) copy-start(f32[256]{0:T(256)} %param.39) | copy-start | bytes 3076
  50.0 5.0 %copy-start.11 = (f32[256]{0:T(256)S(1)}, f32[256]{0:T(256)}, u32[]{:S(2)}) copy-start(f32[256]{0:T(256)} %param.40) | copy-start | bytes 3076
  50.0 5.3 %copy-start.3 = (f32[16,16,128]{2,1,0:T(8,128)S(1)}, f32[16,16,128]{2,1,0:T(8,128)}, u32[]{:S(2)}) copy-start(f32[16,16,128]{2,1,0:T(8,128)} %cost_ref.3) | copy-start | bytes 393220
  50.0 36.7 %all-to-all-start = ((f32[128,34,1,128]{3,2,1,0:T(1,128)}), f32[128,34,1,128]{3,2,1,0:T(1,128)}, u32[]{:S(2)}, u32[]{:S(2)}) async-start(f32[128,34,1,128]{3,2,1,0:T(1,128)} %bitcast.30), calls=%async_computation | async-start | bytes 4456448 | tf_op jit(solution)/shard_map/all_to_all | solution.py:417
  55.3 3.4 %copy-start.5 = (bf16[16,16,128,128]{3,2,1,0:T(8,128)(2,1)S(1)}, bf16[16,16,128,128]{3,2,1,0:T(8,128)(2,1)}, u32[]{:S(2)}) copy-start(bf16[16,16,128,128]{3,2,1,0:T(8,128)(2,1)} %copy-done.4) | copy-start | bytes 25165828
  86.7 39.0 %all-to-all-start.3 = ((f32[128,31,1,128]{3,2,1,0:T(1,128)}), f32[128,31,1,128]{3,2,1,0:T(1,128)S(1)}, u32[]{:S(2)}, u32[]{:S(2)}) async-start(f32[128,31,1,128]{3,2,1,0:T(1,128)} %bitcast.33), calls=%async_computation.3 | async-start | bytes 4063232 | tf_op jit(solution)/shard_map/all_to_all | solution.py:417
  94.9 3.4 %copy-start.6 = (bf16[16,16,128,128]{3,2,1,0:T(8,128)(2,1)S(1)}, bf16[16,16,128,128]{3,2,1,0:T(8,128)(2,1)}, u32[]{:S(2)}) copy-start(bf16[16,16,128,128]{3,2,1,0:T(8,128)(2,1)} %copy-done.4) | copy-start | bytes 25165828
  125.7 39.7 %all-to-all-start.1 = ((f32[128,31,1,128]{3,2,1,0:T(1,128)}), f32[128,31,1,128]{3,2,1,0:T(1,128)}, u32[]{:S(2)}, u32[]{:S(2)}) async-start(f32[128,31,1,128]{3,2,1,0:T(1,128)} %bitcast.32), calls=%async_computation.1 | async-start | bytes 4063232 | tf_op jit(solution)/shard_map/all_to_all | solution.py:417
where the time goes:
time: 172 us
  Pallas kernels  79.6 us (46%)
  waiting for transfers between devices  46.3 us (27%)
  starting transfers between devices  34.7 us (20%)
  local copies, waits for them, and re-layouts  10.3 us (6%)
    pallas_call x2, Pallas kernels, per_device(): call(iterations_kernel, pltpu.HBM((PARTS * OUT_ROWS, LANES), f32), [VM, S...  53.7 us
    all_to_all x4, waiting for transfers between devices, swap(): return lax.all_to_all(parts, EVERY, 0, 0, tiled=True).reshape(-1, LANES)  46.3 us
    all_to_all x4, starting transfers between devices, swap(): return lax.all_to_all(parts, EVERY, 0, 0, tiled=True).reshape(-1, LANES)  34.7 us
    pallas_call x2, Pallas kernels, per_device(): call(functools.partial(pack_kernel, half), pltpu.HBM((PARTS * IN_ROWS, LA...  11.5 us
    unnamed x24, local copies, waits for them, and re-layouts  10 us
    pallas_call x2, Pallas kernels, per_device(): call(functools.partial(unpack_kernel, half), tuple((pltpu.HBM(shape, f32)...  9.4 us
    pallas_call x1, Pallas kernels, per_device(): call(tables_kernel, (pltpu.VMEM((REGIONS, REGIONS, LANES, LANES), jnp.bfl...  4.97 us
  transfers between devices with their start and end apart: 4, of which 3 were waited for; matrix products, arithmetic and copies ran while one was open for 0% of the time, Pallas kernels for 39%

commit v1 on v0

--- a/solution.py
+++ b/solution.py
@@ -44,6 +44,7 @@
 DEPOT_COLUMN = 112
 DEPOT_PITCH = 16
 GROUP = 8
+PIECE = 4
 VOLUME, PRICE, PENALTY, ORDER_COST, HOLDING_COST = range(5)
 
 VMEM_BYTES = 20 * 1024 * 1024
@@ -70,10 +71,6 @@
 
 def in_hbm(array):
     return pltpu.with_memory_space_constraint(array, pltpu.HBM)
-
-
-def in_vmem(array):
-    return pltpu.with_memory_space_constraint(array, pltpu.VMEM)
 
 
 def lane_window(start, size):
@@ -108,20 +105,12 @@
         supply_ref,
     ) = held
     coming = [pltpu.make_async_copy(given[i], held[i], came.at[i]) for i in range(13)]
-    for copy in coming:
+    for copy in (*coming[1:], coming[0]):
         copy.start()
     scen = place_ref[1]
     place = place_ref[0] * SCENARIOS + scen
     cols = slice(half * LANES, (half + 1) * LANES)
 
-    coming[0].wait()
-
-    def ship_step(b, carry):
-        lanes = ship_ref[pl.ds(b * (2 * LANES) + half, LANES, stride=2), :]
-        packed[pl.ds(MAIN + b, PARTS, stride=IN_ROWS), :] = lanes.T
-        return carry
-
-    lax.fori_loop(0, REGIONS, ship_step, 0)
     for copy in coming[1:]:
         copy.wait()
     index[...] = jnp.zeros_like(index)
@@ -162,6 +151,10 @@
                 scen % 2 == 0, supply_ref[:, 0, cols], ordering_ref[:, cols]
             )
         packed[pl.ds(slot, PARTS, stride=IN_ROWS), :] = block[...].T
+    coming[0].wait()
+    for b in range(REGIONS):
+        lanes = ship_ref[pl.ds(b * (2 * LANES) + half, LANES, stride=2), :]
+        packed[pl.ds(MAIN + b, PARTS, stride=IN_ROWS), :] = lanes.T
     going = pltpu.make_async_copy(packed, out_ref, left)
     going.start()
     going.wait()
@@ -177,32 +170,21 @@
     coming = [pltpu.make_async_copy(given[i], earlier[i], came.at[i]) for i in range(len(given))]
     for copy in coming:
         copy.start()
-    going = [pltpu.make_async_copy(held[i], outs[i], left.at[i]) for i in range(count)]
     pace = half + 1
+    going = [pltpu.make_async_copy(held[i], outs[i], left.at[i]) for i in range(1, count)]
+    span = PIECE * LANES * pace
+    pieces = [
+        pltpu.make_async_copy(
+            ship_ref.at[pl.ds(i * span, span)],
+            outs[0].at[pl.ds(i * span, span)],
+            left.at[count + i],
+        )
+        for i in range(REGIONS // PIECE)
+    ]
 
     def get(slot):
         return in_ref[pl.ds(slot, PARTS, stride=OUT_ROWS), :].T
 
-    if half:
-        coming[0].wait()
-
-    def ship_step(b, carry):
-        ship_ref[pl.ds(b * (LANES * pace) + half, LANES, stride=pace), :] = get(OUT_MAIN + b)
-        if half:
-            ship_ref[pl.ds(b * (LANES * pace), LANES, stride=pace), :] = earlier[0][
-                pl.ds(b * LANES, LANES), :
-            ]
-        return carry
-
-    lax.fori_loop(0, REGIONS, ship_step, 0)
-    going[0].start()
-    for copy in coming[1:]:
-        copy.wait()
-    if half:
-        for i, ref in ((1, hold_ref), (2, sell_ref), (3, bal_ref)):
-            ref[pl.ds(0, STORES * AGES, stride=2), :] = earlier[i][...]
-        depot_dual_ref[:, 0, :LANES] = earlier[4][...]
-        ordering_ref[:, :LANES] = earlier[5][...]
     for slot in range(OUT_MAIN):
         ref, age = (hold_ref, sell_ref, bal_ref)[slot // AGES], slot % AGES
         rows = get(slot)
@@ -221,15 +203,29 @@
                 ordering_ref[:, LANES:] = depots
             else:
                 ordering_ref[...] = depots
-    for copy in going[1:]:
+    for copy in coming[1:]:
+        copy.wait()
+    if half:
+        for i, ref in ((1, hold_ref), (2, sell_ref), (3, bal_ref)):
+            ref[pl.ds(0, STORES * AGES, stride=2), :] = earlier[i][...]
+        depot_dual_ref[:, 0, :LANES] = earlier[4][...]
+        ordering_ref[:, :LANES] = earlier[5][...]
+    for copy in going:
         copy.start()
-    for copy in going:
+    if half:
+        coming[0].wait()
+    for b in range(REGIONS):
+        at = b * (LANES * pace)
+        ship_ref[pl.ds(at + half, LANES, stride=pace), :] = get(OUT_MAIN + b)
+        if half:
+            ship_ref[pl.ds(at, LANES, stride=pace), :] = earlier[0][b * LANES : (b + 1) * LANES, :]
+        if b % PIECE == PIECE - 1:
+            pieces[b // PIECE].start()
+    for copy in (*going, *pieces):
         copy.wait()
 
 
-def tables_kernel(
-    place_ref, store_ref, depot_ref, mask_ref, table_ref, slot_ref, keep_ref, next_ref
-):
+def tables_kernel(place_ref, store_ref, depot_ref, mask_ref, out_ref, next_ref, table, left):
     for i in range(2):
         next_ref[i] = place_ref[i]
     column = lax.broadcasted_iota(jnp.int32, (LANES, LANES), 0)
@@ -240,34 +236,27 @@
             store = jnp.where(keep, store_ref[a, pl.ds(b, 1), :], -1)
             depot = jnp.where(keep, depot_ref[a, pl.ds(b, 1), :] + DEPOT_COLUMN, -1)
             ends = (column == store) | (column == depot)
-            table_ref[b, a] = jnp.where(ends, 1.0, 0.0).astype(f32).T.astype(jnp.bfloat16)
+            table[b // 2, b % 2, a] = jnp.where(ends, 1.0, 0.0).astype(f32).T.astype(jnp.bfloat16)
         return carry
 
     lax.fori_loop(0, REGIONS, step, 0)
-    for a in range(REGIONS):
-        slot_ref[a] = depot_ref[a] + (a % GROUP) * DEPOT_PITCH
-        keep_ref[a] = mask_ref[a].astype(f32)
-
-
-def iterations_kernel(
-    in_ref,
-    number_ref,
-    table_ref,
-    store_ref,
-    slot_ref,
-    cost_ref,
-    keep_ref,
-    out_ref,
-    ship,
-    main,
-    aux,
-    flow,
-    dual,
-    ordering,
-    supply,
-    packed,
-    left,
-):
+    going = pltpu.make_async_copy(table, out_ref, left)
+    going.start()
+    going.wait()
+
+
+def iterations_kernel(in_ref, number_ref, table_in, *refs):
+    lanes_in, out_ref, table, lanes = refs[:4], refs[4], refs[5], refs[6:10]
+    slots, keeps, ship, main, aux, flow, dual, ordering, supply, packed, came, left = refs[10:]
+    store_ref, depot_ref, mask_ref, cost_ref = lanes
+    tables = [
+        pltpu.make_async_copy(table_in.at[i], table.at[i], came.at[i]) for i in range(REGIONS // 2)
+    ]
+    coming = [
+        pltpu.make_async_copy(lanes_in[i], lanes[i], came.at[REGIONS // 2 + i]) for i in range(4)
+    ]
+    for copy in (*coming, *tables):
+        copy.start()
     sublane = lax.broadcasted_iota(jnp.int32, (ROWS, LANES), 0)
     first_day = sublane < SCENARIOS
     even = sublane % 2 == 0
@@ -302,6 +291,11 @@
         supply[group] = jnp.where(even, mixed, pltpu.roll(mixed, 1, 0))
         ordering[group] = jnp.where(even, pltpu.roll(mixed, ROWS - 1, 0), mixed)
 
+    for copy in coming:
+        copy.wait()
+    for a in range(REGIONS):
+        slots[a] = depot_ref[a] + (a % GROUP) * DEPOT_PITCH
+        keeps[a] = mask_ref[a].astype(f32)
     volume, price, penalty, order_cost = (number_ref[i] for i in range(4))
     holding_cost = [number_ref[HOLDING_COST + age] for age in range(AGES)]
 
@@ -311,7 +305,7 @@
             dual[group] + jnp.where(first_day, other_day(dual[group]), 0.0) for group in range(2)
         ]
 
-        def step(b, carry):
+        def store_step(b):
             bal = [main[b, BAL + age] for age in range(AGES)]
             ddual, short = aux[b, DDUAL], aux[b, SHORT]
             new_short = jnp.maximum(0.0, short - PRIMAL_STEP * (penalty - ddual))
@@ -338,32 +332,46 @@
                 before = hold_bar
             short_bar = 2.0 * new_short - short
             aux[b, DDUAL] = ddual + DUAL_STEP * (aux[b, DEMAND] - sold - short_bar)
-            arrived = zero
+            return bal[0], ended
+
+        def step(pair, carry):
+            @pl.when(iteration == 0)
+            def _():
+                pltpu.make_async_copy(table_in.at[pair], table.at[pair], came.at[pair]).wait()
+
+            stores = [store_step(2 * pair + i) for i in range(2)]
+            arrived = [zero, zero]
             for a in range(REGIONS):
-                def spread(ref):
-                    return jnp.broadcast_to(ref[a, pl.ds(b, 1), :], (ROWS, LANES))
-
-                ends = jnp.take_along_axis(
-                    bal[0], spread(store_ref), axis=1, mode="promise_in_bounds"
-                ) + jnp.take_along_axis(
-                    later[a // GROUP], spread(slot_ref), axis=1, mode="promise_in_bounds"
-                )
-                old = ship[a, b]
-                new = spread(keep_ref) * jnp.maximum(
-                    0.0, old - PRIMAL_STEP * (spread(cost_ref) * volume + ends)
-                )
-                ship[a, b] = new
-                bar = 2.0 * new - old
-                high = bar.astype(jnp.bfloat16).astype(f32)
-                parts = jnp.concatenate([high, bar - high], axis=0).astype(jnp.bfloat16)
-                sums = jnp.dot(parts, table_ref[b, a], preferred_element_type=f32)
-                sums = sums[:ROWS] + sums[ROWS:]
-                flow[a] = flow[a] + sums
-                arrived = arrived + sums
-            main[b, BAL] = ended + DUAL_STEP * arrived
+                total = None
+                for i in range(2):
+                    b = 2 * pair + i
+
+                    def spread(ref):
+                        return jnp.broadcast_to(ref[a, pl.ds(b, 1), :], (ROWS, LANES))
+
+                    ends = jnp.take_along_axis(
+                        stores[i][0], spread(store_ref), axis=1, mode="promise_in_bounds"
+                    ) + jnp.take_along_axis(
+                        later[a // GROUP], spread(slots), axis=1, mode="promise_in_bounds"
+                    )
+                    old = ship[a, b]
+                    new = spread(keeps) * jnp.maximum(
+                        0.0, old - PRIMAL_STEP * (spread(cost_ref) * volume + ends)
+                    )
+                    ship[a, b] = new
+                    bar = 2.0 * new - old
+                    high = bar.astype(jnp.bfloat16).astype(f32)
+                    parts = jnp.concatenate([high, bar - high], axis=0).astype(jnp.bfloat16)
+                    sums = jnp.dot(parts, table[pair, i, a], preferred_element_type=f32)
+                    sums = sums[:ROWS] + sums[ROWS:]
+                    arrived[i] = arrived[i] + sums
+                    total = sums if i == 0 else total + sums
+                flow[a] = flow[a] + total
+            for i in range(2):
+                main[2 * pair + i, BAL] = stores[i][1] + DUAL_STEP * arrived[i]
             return carry
 
-        lax.fori_loop(0, REGIONS, step, 0)
+        lax.fori_loop(0, REGIONS // 2, step, 0)
         for group in range(2):
             total = dual[group]
             for shift in (4, 2, 1):
@@ -457,6 +465,8 @@
         ordering_init,
         depot_supply,
     )
+    table_shape = (REGIONS // 2, 2, REGIONS, LANES, LANES)
+    tiles = (REGIONS, REGIONS, LANES)
     arrived = []
     for half in range(HALVES):
         packed = call(
@@ -476,17 +486,12 @@
         )(place, *(in_hbm(array) for array in given))
         arrived.append(swap(packed))
         if half == 0:
-            slots = (REGIONS, REGIONS, LANES)
-            table, slot, keep, place = call(
+            table, place = call(
                 tables_kernel,
-                (
-                    pltpu.VMEM((REGIONS, REGIONS, LANES, LANES), jnp.bfloat16),
-                    pltpu.VMEM(slots, jnp.int32),
-                    pltpu.VMEM(slots, f32),
-                    jax.ShapeDtypeStruct((2,), jnp.int32),
-                ),
+                (pltpu.HBM(table_shape, jnp.bfloat16), jax.ShapeDtypeStruct((2,), jnp.int32)),
                 [SM, VM, VM, VM],
-                (VM, VM, VM, SM),
+                (HB, SM),
+                scratch=[pltpu.VMEM(table_shape, jnp.bfloat16), pltpu.SemaphoreType.DMA],
                 micros=5,
             )(place, lane_store, lane_depot, lane_mask)
     numbers = jnp.concatenate(
@@ -502,9 +507,14 @@
                 call(
                     iterations_kernel,
                     pltpu.HBM((PARTS * OUT_ROWS, LANES), f32),
-                    [VM, SM] + [VM] * 5,
+                    [VM, SM] + [HB] * 5,
                     HB,
                     scratch=[
+                        pltpu.VMEM(table_shape, jnp.bfloat16),
+                        *[pltpu.VMEM(tiles, jnp.int32)] * 3,
+                        pltpu.VMEM(tiles, f32),
+                        pltpu.VMEM(tiles, jnp.int32),
+                        pltpu.VMEM(tiles, f32),
                         pltpu.VMEM((REGIONS, REGIONS, ROWS, LANES), f32),
                         pltpu.VMEM((REGIONS, MAIN, ROWS, LANES), f32),
                         pltpu.VMEM((REGIONS, AUX, ROWS, LANES), f32),
@@ -513,17 +523,17 @@
                         pltpu.VMEM((2, ROWS, LANES), f32),
                         pltpu.VMEM((2, ROWS, LANES), f32),
                         pltpu.VMEM((PARTS * OUT_ROWS, LANES), f32),
+                        pltpu.SemaphoreType.DMA((REGIONS // 2 + 4,)),
                         pltpu.SemaphoreType.DMA,
                     ],
                     micros=20,
                 )(
                     arrived[half],
                     mine.reshape(-1),
-                    in_vmem(table),
-                    lane_store,
-                    in_vmem(slot),
-                    lane_cost,
-                    in_vmem(keep),
+                    *(
+                        in_hbm(array)
+                        for array in (table, lane_store, lane_depot, lane_mask, lane_cost)
+                    ),
                 )
             )
         )
@@ -549,7 +559,7 @@
                 *(pltpu.VMEM(shape, f32) for shape in shapes),
                 *(pltpu.VMEM(array.shape, f32) for array in done),
                 pltpu.SemaphoreType.DMA((count,)),
-                pltpu.SemaphoreType.DMA((count,)),
+                pltpu.SemaphoreType.DMA((count + REGIONS // PIECE,)),
             ],
             micros=4,
         )(back[half], *(in_hbm(array) for array in done))

time: 172 us -> 160 us (0.930)
  waiting for transfers between devices: 46.3 us -> 66.5 us
  Pallas kernels: 79.6 us -> 66.6 us
  local copies, waits for them, and re-layouts: 10.3 us -> 0.34 us
  starting transfers between devices: 34.7 us -> 24.9 us
    all_to_all x4, waiting for transfers between devices: 46.3 us -> 66.5 us  [swap(): return lax.all_to_all(parts, EVERY, 0, 0, tiled=True).reshape(-1, LANES)]
    pallas_call x2, Pallas kernels: 53.7 us -> 41.6 us  [per_device(): call(iterations_kernel, pltpu.HBM((PARTS * OUT_ROWS, LANES), f32), [VM, S...]
    unnamed x24 -> x16, local copies, waits for them, and re-layouts: 10 us -> 0.04 us
    all_to_all x4, starting transfers between devices: 34.7 us -> 24.9 us  [swap(): return lax.all_to_all(parts, EVERY, 0, 0, tiled=True).reshape(-1, LANES)]
    pallas_call x1, Pallas kernels: 4.97 us -> 8.44 us  [per_device(): call(tables_kernel, (pltpu.HBM(table_shape, jnp.bfloat16), jax.ShapeDtype...]
    pallas_call x2, Pallas kernels: 9.4 us -> 6.75 us  [per_device(): call(functools.partial(unpack_kernel, half), tuple((pltpu.HBM(shape, f32)...]
  transfers between devices with their start and end apart: 4 -> 4, of which waited for: 3 -> 4; matrix products, arithmetic and copies ran while one was open for 0% -> 0% of each run, Pallas kernels for 39% -> 36%
where the time goes in v1:
time: 160 us; the launch traced here: 159 us
  Pallas kernels  66.6 us (42%)
  waiting for transfers between devices  66.5 us (42%)
  starting transfers between devices  24.9 us (16%)
    all_to_all x4, waiting for transfers between devices, swap(): return lax.all_to_all(parts, EVERY, 0, 0, tiled=True).reshape(-1, LANES)  66.5 us
    pallas_call x2, Pallas kernels, per_device(): call(iterations_kernel, pltpu.HBM((PARTS * OUT_ROWS, LANES), f32), [VM, S...  41.6 us
    all_to_all x4, starting transfers between devices, swap(): return lax.all_to_all(parts, EVERY, 0, 0, tiled=True).reshape(-1, LANES)  24.9 us
    pallas_call x2, Pallas kernels, per_device(): call(functools.partial(pack_kernel, half), pltpu.HBM((PARTS * IN_ROWS, LA...  9.76 us
    pallas_call x1, Pallas kernels, per_device(): call(tables_kernel, (pltpu.HBM(table_shape, jnp.bfloat16), jax.ShapeDtype...  8.44 us
    pallas_call x2, Pallas kernels, per_device(): call(functools.partial(unpack_kernel, half), tuple((pltpu.HBM(shape, f32)...  6.75 us
  transfers between devices with their start and end apart: 4, of which 4 were waited for; matrix products, arithmetic and copies ran while one was open for 0% of the time, Pallas kernels for 36%

profile of v1, /device:TPU:1, one launch (start us, length us, event | category | flops | bytes accessed | tf_op | source)
XLA Modules:
  0.0 159.2 jit_solution(10764443577804635249)
XLA Ops:
  0.6 0.1 pad_add_fusion.place_ref
  0.7 4.9 %shard_map.256 = f32[4352,128]{1,0:T(8,128)} custom-call(s32[2]{0:T(128)S(1)} %pad_add_fusion.place_ref, f32[4096,128]{1,0:T(8,128)} %bitcast.38, f32[1200,128]{1,0:T(8,128)} %bitcast.40, f32[1200,128]{1,0:T(8,128)} %bitcast.42, f32[1200,128]{1,0:T(8,128)} %bitcast.44, f32[200,128]{1,0:T(8,128)} %bitcast.48, f32[200,128]{1,0:T(8,128)} %bitcast.50, ...), custom_call_target="tpu_custom_call" | custom-call | flops 2000000000 | bytes 12000000 | tf_op jit(solution)/shard_map/pallas_call | solution.py:472
  5.6 0.0 copy-start
  5.6 0.0 copy-start.1
  5.6 0.0 copy-start.2
  5.6 11.5 %all-to-all-start.2 = ((f32[128,34,1,128]{3,2,1,0:T(1,128)}), f32[128,34,1,128]{3,2,1,0:T(1,128)S(1)}, u32[]{:S(2)}, u32[]{:S(2)}) async-start(f32[128,34,1,128]{3,2,1,0:T(1,128)} %bitcast.31), calls=%async_computation.2 | async-start | bytes 4456448 | tf_op jit(solution)/shard_map/all_to_all | solution.py:425
  17.2 0.0 copy-done
  17.2 0.0 copy-done.1
  17.2 0.0 copy-done.2
  17.2 8.4 %shard_map.253 = (bf16[8,2,16,128,128]{4,3,2,1,0:T(8,128)(2,1)}, s32[2]{0:T(128)S(1)}) custom-call(s32[2]{0:T(128)S(1)} %pad_add_fusion.place_ref, s32[16,16,128]{2,1,0:T(8,128)S(1)} %copy-done, s32[16,16,128]{2,1,0:T(8,128)S(1)} %copy-done.1, s32[16,16,128]{2,1,0:T(8,128)S(1)} %copy-done.2), custom_call_target="tpu_custom_call" | custom-call | flops 2500000000 | bytes 15000000 | tf_op jit(solution)/shard_map/pallas_call | solution.py:489
  25.6 4.9 %shard_map.254 = f32[4352,128]{1,0:T(8,128)} custom-call(s32[2]{0:T(128)S(1)} %get-tuple-element.20.place_ref, f32[4096,128]{1,0:T(8,128)} %bitcast.39, f32[1200,128]{1,0:T(8,128)} %bitcast.41, f32[1200,128]{1,0:T(8,128)} %bitcast.43, f32[1200,128]{1,0:T(8,128)} %bitcast.45, f32[200,128]{1,0:T(8,128)} %bitcast.49, f32[200,128]{1,0:T(8,128)} %bitcast.51, ...), custom_call_target="tpu_custom_call" | custom-call | flops 2000000000 | bytes 12000000 | tf_op jit(solution)/shard_map/pallas_call | solution.py:472
  30.5 18.6 %all-to-all-done.2 = f32[128,34,1,128]{3,2,1,0:T(1,128)S(1)} async-done(((f32[128,34,1,128]{3,2,1,0:T(1,128)}), f32[128,34,1,128]{3,2,1,0:T(1,128)S(1)}, u32[]{:S(2)}, u32[]{:S(2)}) %all-to-all-start.2) | async-done | bytes 2228256 | tf_op jit(solution)/shard_map/all_to_all | solution.py:425
  49.1 0.0 copy-start.3
  49.1 0.0 copy-start.4
  49.1 0.0 copy-start.5
  49.1 0.0 copy-start.6
  49.1 0.0 copy-start.7
  49.1 4.9 %all-to-all-start = ((f32[128,34,1,128]{3,2,1,0:T(1,128)}), f32[128,34,1,128]{3,2,1,0:T(1,128)}, u32[]{:S(2)}, u32[]{:S(2)}) async-start(f32[128,34,1,128]{3,2,1,0:T(1,128)} %bitcast.30), calls=%async_computation | async-start | bytes 4456448 | tf_op jit(solution)/shard_map/all_to_all | solution.py:425
  54.1 0.0 copy-done.3
  54.1 0.0 copy-done.4
  54.1 0.0 copy-done.5
  54.1 0.0 copy-done.6
  54.1 0.0 copy-done.7
  54.1 0.1 concatenate.3
  54.2 0.2 dynamic-slice_reduce_fusion
  54.4 20.3 %shard_map.257 = f32[3968,128]{1,0:T(8,128)} custom-call(f32[4352,128]{1,0:T(8,128)S(1)} %bitcast.28, f32[10]{0:T(128)S(1)} %get-tuple-element.52.number_ref, bf16[8,2,16,128,128]{4,3,2,1,0:T(8,128)(2,1)} %get-tuple-element.21.table_in, s32[16,16,128]{2,1,0:T(8,128)} %refs_0_.3, s32[16,16,128]{2,1,0:T(8,128)} %refs_1_.3, s32[16,16,128]{2,1,0:T(8,128)} %refs_2_.3, ...), custom_call_target="tpu_custom_call" | custom-call | flops 10000000000 | bytes 60000000 | tf_op jit(solution)/shard_map/pallas_call | solution.py:507
  74.7 11.2 %all-to-all-done = f32[128,34,1,128]{3,2,1,0:T(1,128)} async-done(((f32[128,34,1,128]{3,2,1,0:T(1,128)}), f32[128,34,1,128]{3,2,1,0:T(1,128)}, u32[]{:S(2)}, u32[]{:S(2)}) %all-to-all-start) | async-done | bytes 2228256 | tf_op jit(solution)/shard_map/all_to_all | solution.py:425
  85.8 3.7 %all-to-all-start.3 = ((f32[128,31,1,128]{3,2,1,0:T(1,128)}), f32[128,31,1,128]{3,2,1,0:T(1,128)S(1)}, u32[]{:S(2)}, u32[]{:S(2)}) async-start(f32[128,31,1,128]{3,2,1,0:T(1,128)} %bitcast.33), calls=%async_computation.3 | async-start | bytes 4063232 | tf_op jit(solution)/shard_map/all_to_all | solution.py:425
  89.6 21.4 %shard_map.255 = f32[3968,128]{1,0:T(8,128)} custom-call(f32[4352,128]{1,0:T(8,128)} %bitcast.12.in_ref, f32[10]{0:T(128)S(1)} %get-tuple-element.53.number_ref, bf16[8,2,16,128,128]{4,3,2,1,0:T(8,128)(2,1)} %get-tuple-element.21.table_in, s32[16,16,128]{2,1,0:T(8,128)} %refs_0_.3, s32[16,16,128]{2,1,0:T(8,128)} %refs_1_.3, s32[16,16,128]{2,1,0:T(8,128)} %refs_2_.3, ...), custom_call_target="tpu_custom_call" | custom-call | flops 10000000000 | bytes 60000000 | tf_op jit(solution)/shard_map/pallas_call | solution.py:507
  111.0 8.6 %all-to-all-done.3 = f32[128,31,1,128]{3,2,1,0:T(1,128)S(1)} async-done(((f32[128,31,1,128]{3,2,1,0:T(1,128)}), f32[128,31,1,128]{3,2,1,0:T(1,128)S(1)}, u32[]{:S(2)}, u32[]{:S(2)}) %all-to-all-start.3) | async-done | bytes 2031648 | tf_op jit(solution)/shard_map/all_to_all | solution.py:425
  119.6 4.8 %all-to-all-start.1 = ((f32[128,31,1,128]{3,2,1,0:T(1,128)}), f32[128,31,1,128]{3,2,1,0:T(1,128)}, u32[]{:S(2)}, u32[]{:S(2)}) async-start(f32[128,31,1,128]{3,2,1,0:T(1,128)} %bitcast.32), calls=%async_computation.1 | async-start | bytes 4063232 | tf_op jit(solution)/shard_map/all_to_all | solution.py:425
  124.4 1.6 %shard_map.258 = (f32[2048,128]{1,0:T(8,128)}, f32[600,128]{1,0:T(8,128)}, f32[600,128]{1,0:T(8,128)}, f32[600,128]{1,0:T(8,128)}, f32[15,128]{1,0:T(8,128)}, /*index=5*/f32[15,128]{1,0:T(8,128)}) custom-call(f32[3968,128]{1,0:T(8,128)S(1)} %bitcast.29), custom_call_target="tpu_custom_call" | custom-call | flops 2000000000 | bytes 12000000 | tf_op jit(solution)/shard_map/pallas_call | solution.py:553
  126.0 28.1 %all-to-all-done.1 = f32[128,31,1,128]{3,2,1,0:T(1,128)} async-done(((f32[128,31,1,128]{3,2,1,0:T(1,128)}), f32[128,31,1,128]{3,2,1,0:T(1,128)}, u32[]{:S(2)}, u32[]{:S(2)}) %all-to-all-start.1) | async-done | bytes 2031648 | tf_op jit(solution)/shard_map/all_to_all | solution.py:425
  154.1 5.1 %shard_map.259 = (f32[4096,128]{1,0:T(8,128)}, f32[1200,128]{1,0:T(8,128)}, f32[1200,128]{1,0:T(8,128)}, f32[1200,128]{1,0:T(8,128)}, f32[15,1,256]{2,1,0:T(1,128)}, /*index=5*/f32[15,256]{1,0:T(8,128)}) custom-call(f32[3968,128]{1,0:T(8,128)} %bitcast.18.in_ref, f32[2048,128]{1,0:T(8,128)} %get-tuple-element.22.refs_0_, ...), custom_call_target="tpu_custom_call" | custom-call | flops 2000000000 | bytes 12000000 | tf_op jit(solution)/shard_map/pallas_call | solution.py:553
Async XLA Ops:
  5.6 11.5 %copy-start = (s32[16,16,128]{2,1,0:T(8,128)S(1)}, s32[16,16,128]{2,1,0:T(8,128)}, u32[]{:S(2)}) copy-start(s32[16,16,128]{2,1,0:T(8,128)} %refs_0_.3) | copy-start | bytes 393220
  5.6 11.5 %copy-start.1 = (s32[16,16,128]{2,1,0:T(8,128)S(1)}, s32[16,16,128]{2,1,0:T(8,128)}, u32[]{:S(2)}) copy-start(s32[16,16,128]{2,1,0:T(8,128)} %refs_1_.3) | copy-start | bytes 393220
  5.6 11.5 %copy-start.2 = (s32[16,16,128]{2,1,0:T(8,128)S(1)}, s32[16,16,128]{2,1,0:T(8,128)}, u32[]{:S(2)}) copy-start(s32[16,16,128]{2,1,0:T(8,128)} %refs_2_.3) | copy-start | bytes 393220
  5.6 43.5 %all-to-all-start.2 = ((f32[128,34,1,128]{3,2,1,0:T(1,128)}), f32[128,34,1,128]{3,2,1,0:T(1,128)S(1)}, u32[]{:S(2)}, u32[]{:S(2)}) async-start(f32[128,34,1,128]{3,2,1,0:T(1,128)} %bitcast.31), calls=%async_computation.2 | async-start | bytes 4456448 | tf_op jit(solution)/shard_map/all_to_all | solution.py:425
  49.1 4.9 %copy-start.3 = (f32[6,256]{1,0:T(8,128)S(1)}, f32[6,256]{1,0:T(8,128)}, u32[]{:S(2)}) copy-start(f32[6,256]{1,0:T(8,128)} %param.37) | copy-start | bytes 18436
  49.1 5.0 %copy-start.4 = (f32[256]{0:T(256)S(1)}, f32[256]{0:T(256)}, u32[]{:S(2)}) copy-start(f32[256]{0:T(256)} %param.36) | copy-start | bytes 3076
  49.1 5.0 %copy-start.5 = (f32[256]{0:T(256)S(1)}, f32[256]{0:T(256)}, u32[]{:S(2)}) copy-start(f32[256]{0:T(256)} %param.38) | copy-start | bytes 3076
  49.1 5.0 %copy-start.6 = (f32[256]{0:T(256)S(1)}, f32[256]{0:T(256)}, u32[]{:S(2)}) copy-start(f32[256]{0:T(256)} %param.39) | copy-start | bytes 3076
  49.1 5.0 %copy-start.7 = (f32[256]{0:T(256)S(1)}, f32[256]{0:T(256)}, u32[]{:S(2)}) copy-start(f32[256]{0:T(256)} %param.40) | copy-start | bytes 3076
  49.1 36.7 %all-to-all-start = ((f32[128,34,1,128]{3,2,1,0:T(1,128)}), f32[128,34,1,128]{3,2,1,0:T(1,128)}, u32[]{:S(2)}, u32[]{:S(2)}) async-start(f32[128,34,1,128]{3,2,1,0:T(1,128)} %bitcast.30), calls=%async_computation | async-start | bytes 4456448 | tf_op jit(solution)/shard_map/all_to_all | solution.py:425
  85.8 33.8 %all-to-all-start.3 = ((f32[128,31,1,128]{3,2,1,0:T(1,128)}), f32[128,31,1,128]{3,2,1,0:T(1,128)S(1)}, u32[]{:S(2)}, u32[]{:S(2)}) async-start(f32[128,31,1,128]{3,2,1,0:T(1,128)} %bitcast.33), calls=%async_computation.3 | async-start | bytes 4063232 | tf_op jit(solution)/shard_map/all_to_all | solution.py:425
  119.6 34.5 %all-to-all-start.1 = ((f32[128,31,1,128]{3,2,1,0:T(1,128)}), f32[128,31,1,128]{3,2,1,0:T(1,128)}, u32[]{:S(2)}, u32[]{:S(2)}) async-start(f32[128,31,1,128]{3,2,1,0:T(1,128)} %bitcast.32), calls=%async_computation.1 | async-start | bytes 4063232 | tf_op jit(solution)/shard_map/all_to_all | solution.py:425

commit v2 on v1

--- a/solution.py
+++ b/solution.py
@@ -30,7 +30,7 @@
 SHORT, DDUAL, DEMAND, STOCK = range(4)
 AUX = 4
 IN_ROWS = MAIN + REGIONS
-OUT_MAIN = 15
+OUT_MAIN = 2 * ITERS - 1
 OUT_ROWS = OUT_MAIN + REGIONS
 SPARE = STORES
 HOSTS = {
@@ -40,7 +40,9 @@
     STOCK: (HOLD + 4, HOLD + 5, SELL + 4, SELL + 5),
 }
 DUAL_HOST, MIXED_HOST = BAL + 4, BAL + 5
-OUT_DUAL_HOST, OUT_ORDER_HOST = 12, 13
+OUT_DUAL_HOST, OUT_ORDER_HOST = ITERS, ITERS + 1
+OWN_SHORT, OWN_DDUAL, OWN_DEMAND = MAIN, MAIN + 1, MAIN + 2
+OWN = MAIN + 3
 DEPOT_COLUMN = 112
 DEPOT_PITCH = 16
 GROUP = 8
@@ -87,8 +89,8 @@
 
 
 def pack_kernel(half, place_ref, *refs):
-    given, out_ref, held = refs[:13], refs[13], refs[14:27]
-    packed, rows, index, came, left = refs[27:]
+    given, out_ref, own_ref, held = refs[:13], refs[13], refs[14], refs[15:28]
+    packed, own, rows, index, came, left = refs[28:]
     (
         ship_ref,
         hold_ref,
@@ -140,7 +142,9 @@
         ref, age = (hold_ref, sell_ref, bal_ref)[slot // AGES], slot % AGES
         block = rows.at[slot]
         block[96:LANES, :] = jnp.zeros((LANES - 96, LANES), f32)
-        block[0:STORES, :] = ref[pl.ds(2 * age + half, STORES, stride=2 * AGES), :]
+        values = ref[pl.ds(2 * age + half, STORES, stride=2 * AGES), :]
+        block[0:STORES, :] = values
+        own[slot * STORES : (slot + 1) * STORES, :] = values
         for kind, hosts in HOSTS.items():
             if slot in hosts:
                 block[SPARE : SPARE + QUARTER, :] = quarter(kind, hosts.index(slot))
@@ -151,24 +155,41 @@
                 scen % 2 == 0, supply_ref[:, 0, cols], ordering_ref[:, cols]
             )
         packed[pl.ds(slot, PARTS, stride=IN_ROWS), :] = block[...].T
+    for slot, values in (
+        (OWN_SHORT, short_ref[pl.ds(half, STORES, stride=2), :]),
+        (OWN_DDUAL, ddual_ref[pl.ds(half, STORES, stride=2), :]),
+        (OWN_DEMAND, demand),
+    ):
+        own[slot * STORES : (slot + 1) * STORES, :] = values
+    kept = pltpu.make_async_copy(own, own_ref, left.at[1])
+    kept.start()
     coming[0].wait()
     for b in range(REGIONS):
         lanes = ship_ref[pl.ds(b * (2 * LANES) + half, LANES, stride=2), :]
         packed[pl.ds(MAIN + b, PARTS, stride=IN_ROWS), :] = lanes.T
-    going = pltpu.make_async_copy(packed, out_ref, left)
+    going = pltpu.make_async_copy(packed, out_ref, left.at[0])
     going.start()
+    kept.wait()
     going.wait()
 
 
-def unpack_kernel(half, in_ref, *refs):
+def unpack_kernel(half, place_ref, in_ref, *refs):
     count = 6
+    local, refs = refs[:3], refs[3:]
     given = refs[: count * half]
     outs = refs[count * half : count * (half + 1)]
     held = refs[count * (half + 1) : count * (half + 2)]
-    *earlier, came, left = refs[count * (half + 2) :]
+    *earlier, both_ref, stock_ref, number_ref, stocks, arrivals, came, left = refs[
+        count * (half + 2) :
+    ]
+    cols = slice(half * LANES, (half + 1) * LANES)
     ship_ref, hold_ref, sell_ref, bal_ref, depot_dual_ref, ordering_ref = held
     coming = [pltpu.make_async_copy(given[i], earlier[i], came.at[i]) for i in range(len(given))]
-    for copy in coming:
+    locals_in = [
+        pltpu.make_async_copy(local[i], ref, came.at[count + i])
+        for i, ref in enumerate((both_ref, stock_ref, number_ref))
+    ]
+    for copy in (*coming, *locals_in):
         copy.start()
     pace = half + 1
     going = [pltpu.make_async_copy(held[i], outs[i], left.at[i]) for i in range(1, count)]
@@ -185,14 +206,29 @@
     def get(slot):
         return in_ref[pl.ds(slot, PARTS, stride=OUT_ROWS), :].T
 
+    if half:
+        coming[0].wait()
+    for b in range(REGIONS):
+        at = b * (LANES * pace)
+        ship_ref[pl.ds(at + half, LANES, stride=pace), :] = get(OUT_MAIN + b)
+        if half:
+            ship_ref[pl.ds(at, LANES, stride=pace), :] = earlier[0][b * LANES : (b + 1) * LANES, :]
+        if b % PIECE == PIECE - 1:
+            pieces[b // PIECE].start()
+    for copy in (*coming[1:], *locals_in):
+        copy.wait()
+    if half:
+        for i, ref in ((1, hold_ref), (2, sell_ref), (3, bal_ref)):
+            ref[pl.ds(0, STORES * AGES, stride=2), :] = earlier[i][...]
+        depot_dual_ref[:, 0, :LANES] = earlier[4][...]
+        ordering_ref[:, :LANES] = earlier[5][...]
     for slot in range(OUT_MAIN):
-        ref, age = (hold_ref, sell_ref, bal_ref)[slot // AGES], slot % AGES
-        rows = get(slot)
-        ref[pl.ds(pace * age + half, STORES, stride=pace * AGES), :] = rows[0:STORES]
-        if slot < 12:
-            at = pace * (AGES * QUARTER * (slot % 4) + 3 + slot // 4) + half
-            bal_ref[pl.ds(at, QUARTER, stride=pace * AGES), :] = rows[SPARE : SPARE + QUARTER]
-        depots = rows[SPARE : SPARE + DEPOTS]
+        arrivals[slot] = get(slot)
+        if slot < 4:
+            arrivals[OUT_MAIN, QUARTER * slot : QUARTER * (slot + 1), :] = arrivals[
+                slot, SPARE : SPARE + QUARTER, :
+            ]
+        depots = arrivals[slot, SPARE : SPARE + DEPOTS, :]
         if slot == OUT_DUAL_HOST:
             if half:
                 depot_dual_ref[:, 0, LANES:] = depots
@@ -203,24 +239,71 @@
                 ordering_ref[:, LANES:] = depots
             else:
                 ordering_ref[...] = depots
-    for copy in coming[1:]:
-        copy.wait()
-    if half:
-        for i, ref in ((1, hold_ref), (2, sell_ref), (3, bal_ref)):
-            ref[pl.ds(0, STORES * AGES, stride=2), :] = earlier[i][...]
-        depot_dual_ref[:, 0, :LANES] = earlier[4][...]
-        ordering_ref[:, :LANES] = earlier[5][...]
+    for age in range(AGES - 1):
+        stocks[age * STORES : (age + 1) * STORES, :] = stock_ref[age, :, cols]
+    first_day = place_ref[0] == 0
+
+    def number(row):
+        return jnp.broadcast_to(number_ref[row : row + 1, cols], (ROWS, LANES))
+
+    def by_day(mine, other):
+        return jnp.where(first_day, mine, other), jnp.where(first_day, other, mine)
+
+    def stores_step(block, carry):
+        at = jnp.minimum(ROWS * block, STORES - ROWS)
+
+        def load(slot):
+            return [
+                both_ref[pl.ds((day * OWN + slot) * STORES + at, ROWS), :] for day in range(DAYS)
+            ]
+
+        hold, sell, bal = (
+            [list(days) for days in zip(*(load(first + age) for age in range(AGES)))]
+            for first in (HOLD, SELL, BAL)
+        )
+        short, ddual, demand = (list(load(slot)) for slot in (OWN_SHORT, OWN_DDUAL, OWN_DEMAND))
+        stock = [stocks[pl.ds(age * STORES + at, ROWS), :] for age in range(AGES - 1)]
+        span = pl.ds(at, ROWS)
+        price, penalty = number(PRICE), number(PENALTY)
+        holding_cost = [number(HOLDING_COST + age) for age in range(AGES)]
+        for iteration in range(ITERS):
+            arrived = by_day(arrivals[iteration, span, :], arrivals[ITERS + iteration, span, :])
+            before, new_bal = None, [None, None]
+            for t in range(DAYS):
+                new_short = jnp.maximum(0.0, short[t] - PRIMAL_STEP * (penalty - ddual[t]))
+                sold, bars, after = None, [], []
+                for age in range(AGES):
+                    here = bal[t][age]
+                    rise = holding_cost[age] - here
+                    if t == 0 and age + 1 < AGES:
+                        rise = rise + bal[1][age + 1]
+                    new_hold = jnp.maximum(0.0, hold[t][age] - PRIMAL_STEP * rise)
+                    new_sell = jnp.maximum(
+                        0.0, sell[t][age] - PRIMAL_STEP * (-price - here - ddual[t])
+                    )
+                    bars.append(2.0 * new_hold - hold[t][age])
+                    sell_bar = 2.0 * new_sell - sell[t][age]
+                    sold = sell_bar if sold is None else sold + sell_bar
+                    hold[t][age], sell[t][age] = new_hold, new_sell
+                    if age == 0:
+                        carried = arrived[t]
+                    else:
+                        carried = before[age - 1] if t else stock[age - 1]
+                    after.append(here - DUAL_STEP * (bars[age] + sell_bar - carried))
+                short_bar = 2.0 * new_short - short[t]
+                ddual[t] = ddual[t] + DUAL_STEP * (demand[t] - sold - short_bar)
+                short[t] = new_short
+                before, new_bal[t] = bars, after
+            bal = new_bal
+        for values, ref in ((hold, hold_ref), (sell, sell_ref), (bal, bal_ref)):
+            for age in range(AGES):
+                rows = pl.ds(pace * (at * AGES + age) + half, ROWS, stride=pace * AGES)
+                ref[rows, :] = jnp.where(first_day, values[0][age], values[1][age])
+        return carry
+
+    lax.fori_loop(0, pl.cdiv(STORES, ROWS), stores_step, 0)
     for copy in going:
         copy.start()
-    if half:
-        coming[0].wait()
-    for b in range(REGIONS):
-        at = b * (LANES * pace)
-        ship_ref[pl.ds(at + half, LANES, stride=pace), :] = get(OUT_MAIN + b)
-        if half:
-            ship_ref[pl.ds(at, LANES, stride=pace), :] = earlier[0][b * LANES : (b + 1) * LANES, :]
-        if b % PIECE == PIECE - 1:
-            pieces[b // PIECE].start()
     for copy in (*going, *pieces):
         copy.wait()
 
@@ -247,7 +330,9 @@
 
 def iterations_kernel(in_ref, number_ref, table_in, *refs):
     lanes_in, out_ref, table, lanes = refs[:4], refs[4], refs[5], refs[6:10]
-    slots, keeps, ship, main, aux, flow, dual, ordering, supply, packed, came, left = refs[10:]
+    slots, keeps, ship, main, aux, arrivals, flow, dual, ordering, supply, packed, came, left = refs[
+        10:
+    ]
     store_ref, depot_ref, mask_ref, cost_ref = lanes
     tables = [
         pltpu.make_async_copy(table_in.at[i], table.at[i], came.at[i]) for i in range(REGIONS // 2)
@@ -369,6 +454,7 @@
                 flow[a] = flow[a] + total
             for i in range(2):
                 main[2 * pair + i, BAL] = stores[i][1] + DUAL_STEP * arrived[i]
+                arrivals[2 * pair + i, iteration] = arrived[i]
             return carry
 
         lax.fori_loop(0, REGIONS // 2, step, 0)
@@ -394,13 +480,16 @@
 
     def fold(region, carry):
         at = region * (ROWS * OUT_ROWS)
-        for slot in range(OUT_MAIN):
-            tile = main[region, slot]
-            if slot < 12:
-                hosted = main[region, BAL + 3 + slot // 4]
-                hosted = shift_lanes(hosted, QUARTER * (slot % 4), SPARE)
-                tile = jnp.where(spares, hosted, tile)
-            packed[pl.ds(at + slot, ROWS, stride=OUT_ROWS), :] = tile
+        rest = other_day(arrivals[region, ITERS - 1])
+        for i in range(ITERS):
+            hosted = shift_lanes(rest, QUARTER * i, SPARE)
+            packed[pl.ds(at + i, ROWS, stride=OUT_ROWS), :] = jnp.where(
+                spares, hosted, arrivals[region, i]
+            )
+            if i + 1 < ITERS:
+                packed[pl.ds(at + ITERS + i, ROWS, stride=OUT_ROWS), :] = other_day(
+                    arrivals[region, i]
+                )
         for b in range(REGIONS):
             packed[pl.ds(at + OUT_MAIN + b, ROWS, stride=OUT_ROWS), :] = ship[region, b]
         return carry
@@ -413,7 +502,7 @@
             for host, ref in ((OUT_DUAL_HOST, dual), (OUT_ORDER_HOST, ordering)):
                 part = shift_lanes(ref[group], i * DEPOT_PITCH, SPARE)
                 packed[pl.ds(at + host, ROWS, stride=OUT_ROWS), :] = jnp.where(
-                    depot_spares, part, main[region, host]
+                    depot_spares, part, other_day(arrivals[region, host - ITERS])
                 )
     going = pltpu.make_async_copy(packed, out_ref, left)
     going.start()
@@ -467,24 +556,27 @@
     )
     table_shape = (REGIONS // 2, 2, REGIONS, LANES, LANES)
     tiles = (REGIONS, REGIONS, LANES)
-    arrived = []
+    start = place
+    arrived, both_days = [], []
     for half in range(HALVES):
-        packed = call(
+        packed, own_stores = call(
             functools.partial(pack_kernel, half),
-            pltpu.HBM((PARTS * IN_ROWS, LANES), f32),
+            (pltpu.HBM((PARTS * IN_ROWS, LANES), f32), pltpu.HBM((OWN * STORES, LANES), f32)),
             [SM] + [HB] * len(given),
-            HB,
+            (HB, HB),
             scratch=[
                 *(pltpu.VMEM(array.shape, array.dtype) for array in given),
                 pltpu.VMEM((PARTS * IN_ROWS, LANES), f32),
+                pltpu.VMEM((OWN * STORES, LANES), f32),
                 pltpu.VMEM((MAIN, LANES, LANES), f32),
                 pltpu.VMEM((8, LANES), jnp.int32),
                 pltpu.SemaphoreType.DMA((len(given),)),
-                pltpu.SemaphoreType.DMA,
+                pltpu.SemaphoreType.DMA((2,)),
             ],
             micros=4,
         )(place, *(in_hbm(array) for array in given))
         arrived.append(swap(packed))
+        both_days.append(lax.all_gather(own_stores, "day", axis=0, tiled=True))
         if half == 0:
             table, place = call(
                 tables_kernel,
@@ -518,6 +610,7 @@
                         pltpu.VMEM((REGIONS, REGIONS, ROWS, LANES), f32),
                         pltpu.VMEM((REGIONS, MAIN, ROWS, LANES), f32),
                         pltpu.VMEM((REGIONS, AUX, ROWS, LANES), f32),
+                        pltpu.VMEM((REGIONS, ITERS, ROWS, LANES), f32),
                         pltpu.VMEM((REGIONS, ROWS, LANES), f32),
                         pltpu.VMEM((2, ROWS, LANES), f32),
                         pltpu.VMEM((2, ROWS, LANES), f32),
@@ -553,16 +646,23 @@
         done = call(
             functools.partial(unpack_kernel, half),
             tuple(pltpu.HBM(shape, f32) for shape in shapes),
-            [VM] + [HB] * len(done),
+            [SM, VM] + [HB] * (3 + len(done)),
             (HB,) * count,
             scratch=[
                 *(pltpu.VMEM(shape, f32) for shape in shapes),
                 *(pltpu.VMEM(array.shape, f32) for array in done),
-                pltpu.SemaphoreType.DMA((count,)),
+                *(pltpu.VMEM(array.shape, f32) for array in (both_days[half], given[9], numbers)),
+                pltpu.VMEM(((AGES - 1) * STORES, LANES), f32),
+                pltpu.VMEM((2 * ITERS, LANES, LANES), f32),
+                pltpu.SemaphoreType.DMA((count + 4,)),
                 pltpu.SemaphoreType.DMA((count + REGIONS // PIECE,)),
             ],
-            micros=4,
-        )(back[half], *(in_hbm(array) for array in done))
+            micros=8,
+        )(
+            start,
+            back[half],
+            *(in_hbm(array) for array in (both_days[half], given[9], numbers, *done)),
+        )
     shipments, holdings, selling, balance, depot_dual, ordering = done
     return (
         shipments.reshape(1, 1, REGIONS, LANES, 1, SKUS),

time: 160 us -> 167 us (1.044)
  waiting for transfers between devices: 66.5 us -> 44.2 us
  between operations: 0.84 us -> 14.3 us
  local copies, waits for them, and re-layouts: 0.34 us -> 9.61 us
  Pallas kernels: 66.6 us -> 71.1 us
  starting transfers between devices: 24.9 us -> 26.7 us
    all_to_all x4, waiting for transfers between devices: 66.5 us -> 42.8 us  [swap(): return lax.all_to_all(parts, EVERY, 0, 0, tiled=True).reshape(-1, LANES)]
    unnamed x16 -> x24, local copies, waits for them, and re-layouts: 0.04 us -> 9.31 us
    pallas_call x2, Pallas kernels: 6.75 us -> 13 us  [per_device(): call(functools.partial(unpack_kernel, half), tuple((pltpu.HBM(shape, f32)...]
    pallas_call x2, Pallas kernels: 41.6 us -> 39.9 us  [per_device(): call(iterations_kernel, pltpu.HBM((PARTS * OUT_ROWS, LANES), f32), [VM, S...]
    all_to_all x4, starting transfers between devices: 24.9 us -> 26.6 us  [swap(): return lax.all_to_all(parts, EVERY, 0, 0, tiled=True).reshape(-1, LANES)]
  transfers between devices with their start and end apart: 4 -> 6, of which waited for: 4 -> 4; matrix products, arithmetic and copies ran while one was open for 0% -> 4% of each run, Pallas kernels for 36% -> 36%
where the time goes in v2:
time: 167 us; the launch traced here: 166 us
  Pallas kernels  71.1 us (43%)
  waiting for transfers between devices  44.2 us (26%)
  starting transfers between devices  26.7 us (16%)
  between operations  14.3 us (9%)
  local copies, waits for them, and re-layouts  9.61 us (6%)
    all_to_all x4, waiting for transfers between devices, swap(): return lax.all_to_all(parts, EVERY, 0, 0, tiled=True).reshape(-1, LANES)  42.8 us
    pallas_call x2, Pallas kernels, per_device(): call(iterations_kernel, pltpu.HBM((PARTS * OUT_ROWS, LANES), f32), [VM, S...  39.9 us
    all_to_all x4, starting transfers between devices, swap(): return lax.all_to_all(parts, EVERY, 0, 0, tiled=True).reshape(-1, LANES)  26.6 us
    pallas_call x2, Pallas kernels, per_device(): call(functools.partial(unpack_kernel, half), tuple((pltpu.HBM(shape, f32)...  13 us
    pallas_call x2, Pallas kernels, per_device(): call(functools.partial(pack_kernel, half), (pltpu.HBM((PARTS * IN_ROWS, L...  9.79 us
    unnamed x24, local copies, waits for them, and re-layouts  9.31 us
    pallas_call x1, Pallas kernels, per_device(): call(tables_kernel, (pltpu.HBM(table_shape, jnp.bfloat16), jax.ShapeDtype...  8.48 us
  transfers between devices with their start and end apart: 6, of which 4 were waited for; matrix products, arithmetic and copies ran while one was open for 4% of the time, Pallas kernels for 36%

profile of v2, /device:TPU:1, one launch (start us, length us, event | category | flops | bytes accessed | tf_op | source)
XLA Modules:
  0.0 166.0 jit_solution(1376353393431128099)
XLA Ops:
  7.2 0.1 pad_add_fusion.place_ref
  7.2 4.9 %shard_map.256 = (f32[4352,128]{1,0:T(8,128)}, f32[2100,128]{1,0:T(8,128)}) custom-call(s32[2]{0:T(128)S(1)} %pad_add_fusion.place_ref, f32[4096,128]{1,0:T(8,128)} %bitcast.43, f32[1200,128]{1,0:T(8,128)} %bitcast.45, f32[1200,128]{1,0:T(8,128)} %bitcast.47, f32[1200,128]{1,0:T(8,128)} %bitcast.49, f32[200,128]{1,0:T(8,128)} %bitcast.55, ...), custom_call_target="tpu_custom_call" | custom-call | flops 2000000000 | bytes 12000000 | tf_op jit(solution)/shard_map/pallas_call | solution.py:562
  12.1 0.0 copy-start.2
  12.2 0.0 copy-start.3
  12.2 0.0 copy-start.4
  12.2 11.5 %all-to-all-start.2 = ((f32[128,34,1,128]{3,2,1,0:T(1,128)}), f32[128,34,1,128]{3,2,1,0:T(1,128)S(1)}, u32[]{:S(2)}, u32[]{:S(2)}) async-start(f32[128,34,1,128]{3,2,1,0:T(1,128)} %bitcast.34), calls=%async_computation.2 | async-start | bytes 4456448 | tf_op jit(solution)/shard_map/all_to_all | solution.py:514
  23.7 0.0 copy-done.2
  23.7 0.0 copy-done.3
  23.7 0.0 copy-done.4
  23.7 8.5 %shard_map.253 = (bf16[8,2,16,128,128]{4,3,2,1,0:T(8,128)(2,1)}, s32[2]{0:T(128)S(1)}) custom-call(s32[2]{0:T(128)S(1)} %pad_add_fusion.place_ref, s32[16,16,128]{2,1,0:T(8,128)S(1)} %copy-done.2, s32[16,16,128]{2,1,0:T(8,128)S(1)} %copy-done.3, s32[16,16,128]{2,1,0:T(8,128)S(1)} %copy-done.4), custom_call_target="tpu_custom_call" | custom-call | flops 2500000000 | bytes 15000000 | tf_op jit(solution)/shard_map/pallas_call | solution.py:581
  32.2 4.9 %shard_map.254 = (f32[4352,128]{1,0:T(8,128)}, f32[2100,128]{1,0:T(8,128)}) custom-call(s32[2]{0:T(128)S(1)} %get-tuple-element.24.place_ref, f32[4096,128]{1,0:T(8,128)} %bitcast.44, f32[1200,128]{1,0:T(8,128)} %bitcast.46, f32[1200,128]{1,0:T(8,128)} %bitcast.48, f32[1200,128]{1,0:T(8,128)} %bitcast.50, f32[200,128]{1,0:T(8,128)} %bitcast.56, ...), custom_call_target="tpu_custom_call" | custom-call | flops 2000000000 | bytes 12000000 | tf_op jit(solution)/shard_map/pallas_call | solution.py:562
  37.1 18.5 %all-to-all-done.2 = f32[128,34,1,128]{3,2,1,0:T(1,128)S(1)} async-done(((f32[128,34,1,128]{3,2,1,0:T(1,128)}), f32[128,34,1,128]{3,2,1,0:T(1,128)S(1)}, u32[]{:S(2)}, u32[]{:S(2)}) %all-to-all-start.2) | async-done | bytes 2228256 | tf_op jit(solution)/shard_map/all_to_all | solution.py:514
  55.6 0.0 copy-start
  55.6 1.4 copy-done
  57.1 0.0 copy-start.6
  57.1 0.0 copy-start.7
  57.1 0.0 copy-start.8
  57.1 0.0 copy-start.9
  57.1 0.0 copy-start.10
  57.1 3.9 %all-to-all-start = ((f32[128,34,1,128]{3,2,1,0:T(1,128)}), f32[128,34,1,128]{3,2,1,0:T(1,128)S(1)}, u32[]{:S(2)}, u32[]{:S(2)}) async-start(f32[128,34,1,128]{3,2,1,0:T(1,128)} %bitcast.33), calls=%async_computation | async-start | bytes 4456448 | tf_op jit(solution)/shard_map/all_to_all | solution.py:514
  61.0 0.0 all-gather.7.cloned.1.call-start
  61.0 0.7 all-gather.7.cloned.1.call-update
  61.7 0.0 copy-done.6
  61.7 0.0 copy-done.7
  61.8 0.0 copy-done.8
  61.8 0.0 copy-done.9
  61.8 0.0 copy-done.10
  61.8 0.1 concatenate.3.refs_2_
  61.9 0.0 copy-start.5
  61.9 0.2 dynamic-slice_reduce_fusion
  62.1 0.0 copy-start.1
  62.1 1.6 copy-done.1
  63.7 19.9 %shard_map.257 = f32[2944,128]{1,0:T(8,128)} custom-call(f32[4352,128]{1,0:T(8,128)S(1)} %bitcast.31, f32[10]{0:T(128)S(1)} %get-tuple-element.60.number_ref, bf16[8,2,16,128,128]{4,3,2,1,0:T(8,128)(2,1)} %get-tuple-element.26.table_in, s32[16,16,128]{2,1,0:T(8,128)} %refs_0_.3, s32[16,16,128]{2,1,0:T(8,128)} %refs_1_.3, s32[16,16,128]{2,1,0:T(8,128)} %refs_2_.3, ...), custom_call_target="tpu_custom_call" | custom-call | flops 10000000000 | bytes 60000000 | tf_op jit(solution)/shard_map/pallas_call | solution.py:599
  83.7 0.0 copy-done.5
  83.7 9.4 %all-to-all-done = f32[128,34,1,128]{3,2,1,0:T(1,128)S(1)} async-done(((f32[128,34,1,128]{3,2,1,0:T(1,128)}), f32[128,34,1,128]{3,2,1,0:T(1,128)S(1)}, u32[]{:S(2)}, u32[]{:S(2)}) %all-to-all-start) | async-done | bytes 2228256 | tf_op jit(solution)/shard_map/all_to_all | solution.py:514
  93.1 4.7 %all-to-all-start.3 = ((f32[128,23,1,128]{3,2,1,0:T(1,128)}), f32[128,23,1,128]{3,2,1,0:T(1,128)}, u32[]{:S(2)}, u32[]{:S(2)}) async-start(f32[128,23,1,128]{3,2,1,0:T(1,128)} %bitcast.36), calls=%async_computation.3 | async-start | bytes 3014656 | tf_op jit(solution)/shard_map/all_to_all | solution.py:514
  97.8 0.0 all-gather.5.cloned.1.call-start
  97.9 0.7 all-gather.5.cloned.1.call-update
  98.6 19.9 %shard_map.255 = f32[2944,128]{1,0:T(8,128)} custom-call(f32[4352,128]{1,0:T(8,128)S(1)} %bitcast.30, f32[10]{0:T(128)S(1)} %get-tuple-element.61.number_ref, bf16[8,2,16,128,128]{4,3,2,1,0:T(8,128)(2,1)} %get-tuple-element.26.table_in, s32[16,16,128]{2,1,0:T(8,128)} %refs_0_.3, s32[16,16,128]{2,1,0:T(8,128)} %refs_1_.3, s32[16,16,128]{2,1,0:T(8,128)} %refs_2_.3, ...), custom_call_target="tpu_custom_call" | custom-call | flops 10000000000 | bytes 60000000 | tf_op jit(solution)/shard_map/pallas_call | solution.py:599
  118.5 3.4 %all-to-all-done.3 = f32[128,23,1,128]{3,2,1,0:T(1,128)} async-done(((f32[128,23,1,128]{3,2,1,0:T(1,128)}), f32[128,23,1,128]{3,2,1,0:T(1,128)}, u32[]{:S(2)}, u32[]{:S(2)}) %all-to-all-start.3) | async-done | bytes 1507360 | tf_op jit(solution)/shard_map/all_to_all | solution.py:514
  121.9 6.5 %all-to-all-start.1 = ((f32[128,23,1,128]{3,2,1,0:T(1,128)}), f32[128,23,1,128]{3,2,1,0:T(1,128)S(1)}, u32[]{:S(2)}, u32[]{:S(2)}) async-start(f32[128,23,1,128]{3,2,1,0:T(1,128)} %bitcast.35), calls=%async_computation.1 | async-start | bytes 3014656 | tf_op jit(solution)/shard_map/all_to_all | solution.py:514
  128.4 0.0 all-gather.7.cloned.1.call-done
  128.5 3.1 %reshape.107.refs_0_ = f32[4200,128]{1,0:T(8,128)} reshape(f32[2,2100,128]{2,1,0:T(8,128)} %all-gather.7.cloned.1.call-done) | data formatting | bytes 4300800
  131.6 0.0 all-gather.5.cloned.1.call-done
  131.6 3.1 %reshape.105.refs_0_ = f32[4200,128]{1,0:T(8,128)} reshape(f32[2,2100,128]{2,1,0:T(8,128)} %all-gather.5.cloned.1.call-done) | data formatting | bytes 4300800
  134.7 6.6 %shard_map.258 = (f32[2048,128]{1,0:T(8,128)}, f32[600,128]{1,0:T(8,128)}, f32[600,128]{1,0:T(8,128)}, f32[600,128]{1,0:T(8,128)}, f32[15,128]{1,0:T(8,128)}, /*index=5*/f32[15,128]{1,0:T(8,128)}) custom-call(s32[2]{0:T(128)S(1)} %pad_add_fusion.place_ref, f32[2944,128]{1,0:T(8,128)} %bitcast.23.in_ref, f32[4200,128]{1,0:T(8,128)} %reshape.107.refs_0_, ...), custom_call_target="tpu_custom_call" | custom-call | flops 4000000000 | bytes 24000000 | tf_op jit(solution)/shard_map/pallas_call | solution.py:646
  141.3 11.4 %all-to-all-done.1 = f32[128,23,1,128]{3,2,1,0:T(1,128)S(1)} async-done(((f32[128,23,1,128]{3,2,1,0:T(1,128)}), f32[128,23,1,128]{3,2,1,0:T(1,128)S(1)}, u32[]{:S(2)}, u32[]{:S(2)}) %all-to-all-start.1) | async-done | bytes 1507360 | tf_op jit(solution)/shard_map/all_to_all | solution.py:514
  152.7 6.4 %shard_map.259 = (f32[4096,128]{1,0:T(8,128)}, f32[1200,128]{1,0:T(8,128)}, f32[1200,128]{1,0:T(8,128)}, f32[1200,128]{1,0:T(8,128)}, f32[15,1,256]{2,1,0:T(1,128)}, /*index=5*/f32[15,256]{1,0:T(8,128)}) custom-call(s32[2]{0:T(128)S(1)} %pad_add_fusion.place_ref, f32[2944,128]{1,0:T(8,128)S(1)} %bitcast.32, f32[4200,128]{1,0:T(8,128)} %reshape.105.refs_0_, ...), custom_call_target="tpu_custom_call" | custom-call | flops 4000000000 | bytes 24000000 | tf_op jit(solution)/shard_map/pallas_call | solution.py:646
Async XLA Ops:
  12.1 11.5 %copy-start.2 = (s32[16,16,128]{2,1,0:T(8,128)S(1)}, s32[16,16,128]{2,1,0:T(8,128)}, u32[]{:S(2)}) copy-start(s32[16,16,128]{2,1,0:T(8,128)} %refs_0_.3) | copy-start | bytes 393220
  12.2 11.5 %copy-start.3 = (s32[16,16,128]{2,1,0:T(8,128)S(1)}, s32[16,16,128]{2,1,0:T(8,128)}, u32[]{:S(2)}) copy-start(s32[16,16,128]{2,1,0:T(8,128)} %refs_1_.3) | copy-start | bytes 393220
  12.2 11.5 %copy-start.4 = (s32[16,16,128]{2,1,0:T(8,128)S(1)}, s32[16,16,128]{2,1,0:T(8,128)}, u32[]{:S(2)}) copy-start(s32[16,16,128]{2,1,0:T(8,128)} %refs_2_.3) | copy-start | bytes 393220
  12.2 43.5 %all-to-all-start.2 = ((f32[128,34,1,128]{3,2,1,0:T(1,128)}), f32[128,34,1,128]{3,2,1,0:T(1,128)S(1)}, u32[]{:S(2)}, u32[]{:S(2)}) async-start(f32[128,34,1,128]{3,2,1,0:T(1,128)} %bitcast.34), calls=%async_computation.2 | async-start | bytes 4456448 | tf_op jit(solution)/shard_map/all_to_all | solution.py:514
  55.6 1.4 copy-start
  57.1 4.7 %copy-start.6 = (f32[6,256]{1,0:T(8,128)S(1)}, f32[6,256]{1,0:T(8,128)}, u32[]{:S(2)}) copy-start(f32[6,256]{1,0:T(8,128)} %param.37) | copy-start | bytes 18436
  57.1 4.7 %copy-start.7 = (f32[256]{0:T(256)S(1)}, f32[256]{0:T(256)}, u32[]{:S(2)}) copy-start(f32[256]{0:T(256)} %param.36) | copy-start | bytes 3076
  57.1 4.7 %copy-start.8 = (f32[256]{0:T(256)S(1)}, f32[256]{0:T(256)}, u32[]{:S(2)}) copy-start(f32[256]{0:T(256)} %param.38) | copy-start | bytes 3076
  57.1 4.7 %copy-start.9 = (f32[256]{0:T(256)S(1)}, f32[256]{0:T(256)}, u32[]{:S(2)}) copy-start(f32[256]{0:T(256)} %param.39) | copy-start | bytes 3076
  57.1 4.7 %copy-start.10 = (f32[256]{0:T(256)S(1)}, f32[256]{0:T(256)}, u32[]{:S(2)}) copy-start(f32[256]{0:T(256)} %param.40) | copy-start | bytes 3076
  57.1 36.0 %all-to-all-start = ((f32[128,34,1,128]{3,2,1,0:T(1,128)}), f32[128,34,1,128]{3,2,1,0:T(1,128)S(1)}, u32[]{:S(2)}, u32[]{:S(2)}) async-start(f32[128,34,1,128]{3,2,1,0:T(1,128)} %bitcast.33), calls=%async_computation | async-start | bytes 4456448 | tf_op jit(solution)/shard_map/all_to_all | solution.py:514
  61.0 67.5 %all-gather.7.cloned.1.call-start = ((), (), s32[]{:S(2)}) async-start(), calls=%async_computation.5 | async-start | bytes 3231744 | tf_op jit(solution)/shard_map/all_gather | solution.py:579
  61.9 21.8 %copy-start.5 = (f32[10,256]{1,0:T(8,128)}, f32[10,256]{1,0:T(8,128)S(1)}, u32[]{:S(2)}) copy-start(f32[10,256]{1,0:T(8,128)S(1)} %concatenate.3.refs_2_) | copy-start | bytes 30724
  62.1 1.6 copy-start.1
  93.1 28.8 %all-to-all-start.3 = ((f32[128,23,1,128]{3,2,1,0:T(1,128)}), f32[128,23,1,128]{3,2,1,0:T(1,128)}, u32[]{:S(2)}, u32[]{:S(2)}) async-start(f32[128,23,1,128]{3,2,1,0:T(1,128)} %bitcast.36), calls=%async_computation.3 | async-start | bytes 3014656 | tf_op jit(solution)/shard_map/all_to_all | solution.py:514
  97.8 33.8 %all-gather.5.cloned.1.call-start = ((), (), s32[]{:S(2)}) async-start(), calls=%async_computation.4 | async-start | bytes 3231744 | tf_op jit(solution)/shard_map/all_gather | solution.py:579
  121.9 30.8 %all-to-all-start.1 = ((f32[128,23,1,128]{3,2,1,0:T(1,128)}), f32[128,23,1,128]{3,2,1,0:T(1,128)S(1)}, u32[]{:S(2)}, u32[]{:S(2)}) async-start(f32[128,23,1,128]{3,2,1,0:T(1,128)} %bitcast.35), calls=%async_computation.1 | async-start | bytes 3014656 | tf_op jit(solution)/shard_map/all_to_all | solution.py:514
Sparse Core Ops, SparseCore 0:
  63.5 15.4 all-gather.6
  100.3 15.4 all-gather.4

commit v3 on v1

--- a/solution.py
+++ b/solution.py
@@ -71,6 +71,10 @@
 
 def in_hbm(array):
     return pltpu.with_memory_space_constraint(array, pltpu.HBM)
+
+
+def in_vmem(array):
+    return pltpu.with_memory_space_constraint(array, pltpu.VMEM)
 
 
 def lane_window(start, size):
@@ -562,7 +566,7 @@
                 pltpu.SemaphoreType.DMA((count + REGIONS // PIECE,)),
             ],
             micros=4,
-        )(back[half], *(in_hbm(array) for array in done))
+        )(in_vmem(back[half]) if half else back[half], *(in_hbm(array) for array in done))
     shipments, holdings, selling, balance, depot_dual, ordering = done
     return (
         shipments.reshape(1, 1, REGIONS, LANES, 1, SKUS),

time: 160 us -> 160 us (level)
  no operation moved by 1% of the time
where the time goes in v3:
time: 160 us; the launch traced here: 159 us
  Pallas kernels  66.6 us (42%)
  waiting for transfers between devices  66.5 us (42%)
  starting transfers between devices  24.9 us (16%)
    all_to_all x4, waiting for transfers between devices, swap(): return lax.all_to_all(parts, EVERY, 0, 0, tiled=True).reshape(-1, LANES)  66.5 us
    pallas_call x2, Pallas kernels, per_device(): call(iterations_kernel, pltpu.HBM((PARTS * OUT_ROWS, LANES), f32), [VM, S...  41.6 us
    all_to_all x4, starting transfers between devices, swap(): return lax.all_to_all(parts, EVERY, 0, 0, tiled=True).reshape(-1, LANES)  24.9 us
    pallas_call x2, Pallas kernels, per_device(): call(functools.partial(pack_kernel, half), pltpu.HBM((PARTS * IN_ROWS, LA...  9.76 us
    pallas_call x1, Pallas kernels, per_device(): call(tables_kernel, (pltpu.HBM(table_shape, jnp.bfloat16), jax.ShapeDtype...  8.44 us
    pallas_call x2, Pallas kernels, per_device(): call(functools.partial(unpack_kernel, half), tuple((pltpu.HBM(shape, f32)...  6.75 us
  transfers between devices with their start and end apart: 4, of which 4 were waited for; matrix products, arithmetic and copies ran while one was open for 0% of the time, Pallas kernels for 36%

profile of v3, /device:TPU:1, one launch (start us, length us, event | category | flops | bytes accessed | tf_op | source)
XLA Modules:
  0.0 159.2 jit_solution(10764443577804635249)
XLA Ops:
  0.6 0.1 pad_add_fusion.place_ref
  0.7 4.9 %shard_map.256 = f32[4352,128]{1,0:T(8,128)} custom-call(s32[2]{0:T(128)S(1)} %pad_add_fusion.place_ref, f32[4096,128]{1,0:T(8,128)} %bitcast.38, f32[1200,128]{1,0:T(8,128)} %bitcast.40, f32[1200,128]{1,0:T(8,128)} %bitcast.42, f32[1200,128]{1,0:T(8,128)} %bitcast.44, f32[200,128]{1,0:T(8,128)} %bitcast.48, f32[200,128]{1,0:T(8,128)} %bitcast.50, ...), custom_call_target="tpu_custom_call" | custom-call | flops 2000000000 | bytes 12000000 | tf_op jit(solution)/shard_map/pallas_call | solution.py:476
  5.6 0.0 copy-start
  5.6 0.0 copy-start.1
  5.6 0.0 copy-start.2
  5.6 11.5 %all-to-all-start.2 = ((f32[128,34,1,128]{3,2,1,0:T(1,128)}), f32[128,34,1,128]{3,2,1,0:T(1,128)S(1)}, u32[]{:S(2)}, u32[]{:S(2)}) async-start(f32[128,34,1,128]{3,2,1,0:T(1,128)} %bitcast.31), calls=%async_computation.2 | async-start | bytes 4456448 | tf_op jit(solution)/shard_map/all_to_all | solution.py:429
  17.2 0.0 copy-done
  17.2 0.0 copy-done.1
  17.2 0.0 copy-done.2
  17.2 8.4 %shard_map.253 = (bf16[8,2,16,128,128]{4,3,2,1,0:T(8,128)(2,1)}, s32[2]{0:T(128)S(1)}) custom-call(s32[2]{0:T(128)S(1)} %pad_add_fusion.place_ref, s32[16,16,128]{2,1,0:T(8,128)S(1)} %copy-done, s32[16,16,128]{2,1,0:T(8,128)S(1)} %copy-done.1, s32[16,16,128]{2,1,0:T(8,128)S(1)} %copy-done.2), custom_call_target="tpu_custom_call" | custom-call | flops 2500000000 | bytes 15000000 | tf_op jit(solution)/shard_map/pallas_call | solution.py:493
  25.6 4.9 %shard_map.254 = f32[4352,128]{1,0:T(8,128)} custom-call(s32[2]{0:T(128)S(1)} %get-tuple-element.20.place_ref, f32[4096,128]{1,0:T(8,128)} %bitcast.39, f32[1200,128]{1,0:T(8,128)} %bitcast.41, f32[1200,128]{1,0:T(8,128)} %bitcast.43, f32[1200,128]{1,0:T(8,128)} %bitcast.45, f32[200,128]{1,0:T(8,128)} %bitcast.49, f32[200,128]{1,0:T(8,128)} %bitcast.51, ...), custom_call_target="tpu_custom_call" | custom-call | flops 2000000000 | bytes 12000000 | tf_op jit(solution)/shard_map/pallas_call | solution.py:476
  30.5 18.6 %all-to-all-done.2 = f32[128,34,1,128]{3,2,1,0:T(1,128)S(1)} async-done(((f32[128,34,1,128]{3,2,1,0:T(1,128)}), f32[128,34,1,128]{3,2,1,0:T(1,128)S(1)}, u32[]{:S(2)}, u32[]{:S(2)}) %all-to-all-start.2) | async-done | bytes 2228256 | tf_op jit(solution)/shard_map/all_to_all | solution.py:429
  49.1 0.0 copy-start.3
  49.1 0.0 copy-start.4
  49.1 0.0 copy-start.5
  49.1 0.0 copy-start.6
  49.1 0.0 copy-start.7
  49.1 4.9 %all-to-all-start = ((f32[128,34,1,128]{3,2,1,0:T(1,128)}), f32[128,34,1,128]{3,2,1,0:T(1,128)}, u32[]{:S(2)}, u32[]{:S(2)}) async-start(f32[128,34,1,128]{3,2,1,0:T(1,128)} %bitcast.30), calls=%async_computation | async-start | bytes 4456448 | tf_op jit(solution)/shard_map/all_to_all | solution.py:429
  54.1 0.0 copy-done.3
  54.1 0.0 copy-done.4
  54.1 0.0 copy-done.5
  54.1 0.0 copy-done.6
  54.1 0.0 copy-done.7
  54.1 0.1 concatenate.3
  54.2 0.2 dynamic-slice_reduce_fusion
  54.4 20.3 %shard_map.257 = f32[3968,128]{1,0:T(8,128)} custom-call(f32[4352,128]{1,0:T(8,128)S(1)} %bitcast.28, f32[10]{0:T(128)S(1)} %get-tuple-element.52.number_ref, bf16[8,2,16,128,128]{4,3,2,1,0:T(8,128)(2,1)} %get-tuple-element.21.table_in, s32[16,16,128]{2,1,0:T(8,128)} %refs_0_.3, s32[16,16,128]{2,1,0:T(8,128)} %refs_1_.3, s32[16,16,128]{2,1,0:T(8,128)} %refs_2_.3, ...), custom_call_target="tpu_custom_call" | custom-call | flops 10000000000 | bytes 60000000 | tf_op jit(solution)/shard_map/pallas_call | solution.py:511
  74.7 11.2 %all-to-all-done = f32[128,34,1,128]{3,2,1,0:T(1,128)} async-done(((f32[128,34,1,128]{3,2,1,0:T(1,128)}), f32[128,34,1,128]{3,2,1,0:T(1,128)}, u32[]{:S(2)}, u32[]{:S(2)}) %all-to-all-start) | async-done | bytes 2228256 | tf_op jit(solution)/shard_map/all_to_all | solution.py:429
  85.8 3.7 %all-to-all-start.3 = ((f32[128,31,1,128]{3,2,1,0:T(1,128)}), f32[128,31,1,128]{3,2,1,0:T(1,128)S(1)}, u32[]{:S(2)}, u32[]{:S(2)}) async-start(f32[128,31,1,128]{3,2,1,0:T(1,128)} %bitcast.33), calls=%async_computation.3 | async-start | bytes 4063232 | tf_op jit(solution)/shard_map/all_to_all | solution.py:429
  89.6 21.4 %shard_map.255 = f32[3968,128]{1,0:T(8,128)} custom-call(f32[4352,128]{1,0:T(8,128)} %bitcast.12.in_ref, f32[10]{0:T(128)S(1)} %get-tuple-element.53.number_ref, bf16[8,2,16,128,128]{4,3,2,1,0:T(8,128)(2,1)} %get-tuple-element.21.table_in, s32[16,16,128]{2,1,0:T(8,128)} %refs_0_.3, s32[16,16,128]{2,1,0:T(8,128)} %refs_1_.3, s32[16,16,128]{2,1,0:T(8,128)} %refs_2_.3, ...), custom_call_target="tpu_custom_call" | custom-call | flops 10000000000 | bytes 60000000 | tf_op jit(solution)/shard_map/pallas_call | solution.py:511
  111.0 8.6 %all-to-all-done.3 = f32[128,31,1,128]{3,2,1,0:T(1,128)S(1)} async-done(((f32[128,31,1,128]{3,2,1,0:T(1,128)}), f32[128,31,1,128]{3,2,1,0:T(1,128)S(1)}, u32[]{:S(2)}, u32[]{:S(2)}) %all-to-all-start.3) | async-done | bytes 2031648 | tf_op jit(solution)/shard_map/all_to_all | solution.py:429
  119.6 4.8 %all-to-all-start.1 = ((f32[128,31,1,128]{3,2,1,0:T(1,128)}), f32[128,31,1,128]{3,2,1,0:T(1,128)}, u32[]{:S(2)}, u32[]{:S(2)}) async-start(f32[128,31,1,128]{3,2,1,0:T(1,128)} %bitcast.32), calls=%async_computation.1 | async-start | bytes 4063232 | tf_op jit(solution)/shard_map/all_to_all | solution.py:429
  124.4 1.6 %shard_map.258 = (f32[2048,128]{1,0:T(8,128)}, f32[600,128]{1,0:T(8,128)}, f32[600,128]{1,0:T(8,128)}, f32[600,128]{1,0:T(8,128)}, f32[15,128]{1,0:T(8,128)}, /*index=5*/f32[15,128]{1,0:T(8,128)}) custom-call(f32[3968,128]{1,0:T(8,128)S(1)} %bitcast.29), custom_call_target="tpu_custom_call" | custom-call | flops 2000000000 | bytes 12000000 | tf_op jit(solution)/shard_map/pallas_call | solution.py:557
  126.0 28.1 %all-to-all-done.1 = f32[128,31,1,128]{3,2,1,0:T(1,128)} async-done(((f32[128,31,1,128]{3,2,1,0:T(1,128)}), f32[128,31,1,128]{3,2,1,0:T(1,128)}, u32[]{:S(2)}, u32[]{:S(2)}) %all-to-all-start.1) | async-done | bytes 2031648 | tf_op jit(solution)/shard_map/all_to_all | solution.py:429
  154.1 5.1 %shard_map.259 = (f32[4096,128]{1,0:T(8,128)}, f32[1200,128]{1,0:T(8,128)}, f32[1200,128]{1,0:T(8,128)}, f32[1200,128]{1,0:T(8,128)}, f32[15,1,256]{2,1,0:T(1,128)}, /*index=5*/f32[15,256]{1,0:T(8,128)}) custom-call(f32[3968,128]{1,0:T(8,128)} %bitcast.18.in_ref, f32[2048,128]{1,0:T(8,128)} %get-tuple-element.22.refs_0_, ...), custom_call_target="tpu_custom_call" | custom-call | flops 2000000000 | bytes 12000000 | tf_op jit(solution)/shard_map/pallas_call | solution.py:557
Async XLA Ops:
  5.6 11.5 %copy-start = (s32[16,16,128]{2,1,0:T(8,128)S(1)}, s32[16,16,128]{2,1,0:T(8,128)}, u32[]{:S(2)}) copy-start(s32[16,16,128]{2,1,0:T(8,128)} %refs_0_.3) | copy-start | bytes 393220
  5.6 11.5 %copy-start.1 = (s32[16,16,128]{2,1,0:T(8,128)S(1)}, s32[16,16,128]{2,1,0:T(8,128)}, u32[]{:S(2)}) copy-start(s32[16,16,128]{2,1,0:T(8,128)} %refs_1_.3) | copy-start | bytes 393220
  5.6 11.5 %copy-start.2 = (s32[16,16,128]{2,1,0:T(8,128)S(1)}, s32[16,16,128]{2,1,0:T(8,128)}, u32[]{:S(2)}) copy-start(s32[16,16,128]{2,1,0:T(8,128)} %refs_2_.3) | copy-start | bytes 393220
  5.6 43.5 %all-to-all-start.2 = ((f32[128,34,1,128]{3,2,1,0:T(1,128)}), f32[128,34,1,128]{3,2,1,0:T(1,128)S(1)}, u32[]{:S(2)}, u32[]{:S(2)}) async-start(f32[128,34,1,128]{3,2,1,0:T(1,128)} %bitcast.31), calls=%async_computation.2 | async-start | bytes 4456448 | tf_op jit(solution)/shard_map/all_to_all | solution.py:429
  49.1 4.9 %copy-start.3 = (f32[6,256]{1,0:T(8,128)S(1)}, f32[6,256]{1,0:T(8,128)}, u32[]{:S(2)}) copy-start(f32[6,256]{1,0:T(8,128)} %param.37) | copy-start | bytes 18436
  49.1 5.0 %copy-start.4 = (f32[256]{0:T(256)S(1)}, f32[256]{0:T(256)}, u32[]{:S(2)}) copy-start(f32[256]{0:T(256)} %param.36) | copy-start | bytes 3076
  49.1 5.0 %copy-start.5 = (f32[256]{0:T(256)S(1)}, f32[256]{0:T(256)}, u32[]{:S(2)}) copy-start(f32[256]{0:T(256)} %param.38) | copy-start | bytes 3076
  49.1 5.0 %copy-start.6 = (f32[256]{0:T(256)S(1)}, f32[256]{0:T(256)}, u32[]{:S(2)}) copy-start(f32[256]{0:T(256)} %param.39) | copy-start | bytes 3076
  49.1 5.0 %copy-start.7 = (f32[256]{0:T(256)S(1)}, f32[256]{0:T(256)}, u32[]{:S(2)}) copy-start(f32[256]{0:T(256)} %param.40) | copy-start | bytes 3076
  49.1 36.7 %all-to-all-start = ((f32[128,34,1,128]{3,2,1,0:T(1,128)}), f32[128,34,1,128]{3,2,1,0:T(1,128)}, u32[]{:S(2)}, u32[]{:S(2)}) async-start(f32[128,34,1,128]{3,2,1,0:T(1,128)} %bitcast.30), calls=%async_computation | async-start | bytes 4456448 | tf_op jit(solution)/shard_map/all_to_all | solution.py:429
  85.8 33.8 %all-to-all-start.3 = ((f32[128,31,1,128]{3,2,1,0:T(1,128)}), f32[128,31,1,128]{3,2,1,0:T(1,128)S(1)}, u32[]{:S(2)}, u32[]{:S(2)}) async-start(f32[128,31,1,128]{3,2,1,0:T(1,128)} %bitcast.33), calls=%async_computation.3 | async-start | bytes 4063232 | tf_op jit(solution)/shard_map/all_to_all | solution.py:429
  119.6 34.5 %all-to-all-start.1 = ((f32[128,31,1,128]{3,2,1,0:T(1,128)}), f32[128,31,1,128]{3,2,1,0:T(1,128)}, u32[]{:S(2)}, u32[]{:S(2)}) async-start(f32[128,31,1,128]{3,2,1,0:T(1,128)} %bitcast.32), calls=%async_computation.1 | async-start | bytes 4063232 | tf_op jit(solution)/shard_map/all_to_all | solution.py:429
